TPU v7x, 256 devices: a whole 4x4x8 slice. The times are simulated.
256 devices in a mesh: dp: 32 (over z, y), tensor: 8 (over x, core).
Axes of the slice: x: 4, y: 4, z: 8, core: 2. Of those that a mesh axis runs over, the one named last changes fastest.
Arguments:
- tokens: bfloat16 [2, 512, 12288], P(None, 'dp', 'tensor'), may hold values from -6 to 6
- up_weight: bfloat16 [12288, 49152], P('tensor', 'dp'), may hold values from -0.0546875 to 0.0546875
- up_bias: bfloat16 [49152], P('dp'), may hold values from -3 to 3
- down_weight: bfloat16 [49152, 12288], P('dp', 'tensor'), may hold values from -0.02734375 to 0.02734375
- down_bias: bfloat16 [12288], P('tensor'), may hold values from -3 to 3
- active: int32 [2, 4, 384], P(None, None, 'dp'), may hold values from 0 to 1
Outputs:
- mixed: bfloat16 [2, 512, 12288], P(None, 'dp', 'tensor')
All inputs are finite; a program needn't handle non-finite values.
Results may differ from a plain program's by a relative error of at most 0.0042.
Values may be sent and summed in bfloat16 or wider, within the bound.
No kernel may reach another device: no remote copies, remote signals or barrier semaphores. Data moves between devices by JAX's collectives and lax.ppermute only.
A program may use at most 64 MiB of HBM per device.

v0:
```python
import jax
import jax.numpy as jnp
from jax import lax
from jax.sharding import PartitionSpec as P

RBLK = 128


def activate(summed, up_bias, mask_table):
    row_count = summed.shape[0]
    blocks = mask_table.shape[1]
    row_ids = jnp.arange(row_count, dtype=jnp.int32)
    onehot = (
        row_ids[:, None] // RBLK == jnp.arange(mask_table.shape[0], dtype=jnp.int32)[None, :]
    ).astype(jnp.float32)
    row_mask = jnp.dot(onehot, mask_table.astype(jnp.float32))
    preact = jnp.maximum(summed + up_bias.astype(jnp.float32), 0.0)
    gated_rows = preact.reshape(row_count, blocks, -1) * row_mask[:, :, None]
    return gated_rows.reshape(row_count, -1).astype(jnp.bfloat16)


def local(tokens, up_weight, up_bias, down_weight, down_bias, active):
    results = []
    for step_index in range(tokens.shape[0]):
        local_rows = tokens[step_index]
        mask_table = active[step_index]
        partial_up = jnp.dot(
            lax.all_gather(local_rows, "dp", axis=0, tiled=True),
            up_weight,
            preferred_element_type=jnp.float32,
        )
        summed = lax.psum(partial_up, "tensor")
        hidden = activate(summed, up_bias, mask_table)
        mixed_rows = lax.psum_scatter(
            jnp.dot(hidden, down_weight, preferred_element_type=jnp.float32),
            "dp",
            scatter_dimension=0,
            tiled=True,
        )
        results.append((mixed_rows + down_bias.astype(jnp.float32)).astype(jnp.bfloat16))
    return jnp.stack(results)


def solution(mesh):
    placed = (
        P(None, "dp", "tensor"),
        P("tensor", "dp"),
        P("dp"),
        P("dp", "tensor"),
        P("tensor"),
        P(None, None, "dp"),
    )
    return jax.shard_map(
        local, mesh=mesh, in_specs=placed, out_specs=P(None, "dp", "tensor"), check_vma=False
    )
```

profile of v0, /device:TPU:6, one launch (start us, length us, event | category | flops | bytes accessed | tf_op | source)
XLA Modules:
  0.0 721.4 jit_solution(4117240962509193878)
XLA Ops:
  6.5 1.5 fusion.21
  8.0 0.0 all-gather.7.cloned.1.call-update
  8.0 0.0 all-gather.5.cloned.1.call-start
  8.1 0.7 all-gather.5.cloned.1.call-update
  8.8 0.0 all-reduce.3.cloned.1.call-start
  8.8 81.3 %all-gather.7.cloned.1.call-done = bf16[1,512,1536]{2,1,0:T(8,128)(2,1)} async-done(((bf16[1,16,1536]{2,1,0:T(8,128)(2,1)}), bf16[1,512,1536]{2,1,0:T(8,128)(2,1)}) %all-gather.7.cloned.1.call-update) | async-done | bytes 1572880 | tf_op jit(solution)/shard_map/all_gather | solution.py:28
  90.2 7.1 fusion.2
  97.3 70.2 %all-gather.5.cloned.1.call-done = bf16[1,512,1536]{2,1,0:T(8,128)(2,1)} async-done(((bf16[1,16,1536]{2,1,0:T(8,128)(2,1)}), bf16[1,512,1536]{2,1,0:T(8,128)(2,1)}) %all-gather.5.cloned.1.call-update) | async-done | bytes 1572880 | tf_op jit(solution)/shard_map/all_gather | solution.py:28
  167.4 7.1 fusion.4
  174.6 0.0 all-reduce.3.cloned.1.call-update
  174.6 0.0 reduce-scatter.3.cloned.1.call-start
  174.6 0.6 copy-done
  175.3 0.3 fusion.6
  175.5 0.3 fusion.7
  175.8 84.0 %all-reduce.3.cloned.1.call-done = (f32[512,1536]{0,1:T(8,128)}, f32[512,1536]{0,1:T(8,128)}) async-done(((f32[512,1536]{0,1:T(8,128)}, f32[512,1536]{0,1:T(8,128)}), (f32[512,1536]{0,1:T(8,128)}, f32[512,1536]{0,1:T(8,128)})) %all-reduce.3.cloned.1.call-update) | async-done | bytes 6291472 | tf_op jit(solution)/shard_map/psum | solution.py:32
  259.8 3.6 fusion.1
  263.4 6.6 fusion.22
  270.1 0.0 reduce-scatter.5.cloned.1.call-start
  270.1 6.6 fusion.23
  276.8 0.7 copy-done.1
  277.4 214.0 %reduce-scatter.3.cloned.1.call-done = f32[16,1536]{1,0:T(8,128)} async-done(((f32[512,1536]{1,0:T(8,128)}), f32[16,1536]{1,0:T(8,128)}) %reduce-scatter.3.cloned.1.call-update) | async-done | bytes 98320 | tf_op jit(solution)/shard_map/reduce_scatter | solution.py:34
  491.4 221.9 %reduce-scatter.5.cloned.1.call-done = f32[16,1536]{1,0:T(8,128)} async-done(((f32[512,1536]{1,0:T(8,128)}), f32[16,1536]{1,0:T(8,128)}) %reduce-scatter.5.cloned.1.call-update) | async-done | bytes 98320 | tf_op jit(solution)/shard_map/reduce_scatter | solution.py:34
  713.3 1.0 fusion.10
  714.2 0.7 pad_maximum_fusion
  (10 shorter events, 0.1 us)
Async XLA Ops:
  6.5 83.6 %all-gather.7.cloned.1.call-start = ((), (), s32[]{:S(2)}) async-start(), calls=%async_computation.5 | async-start | bytes 1622016 | tf_op jit(solution)/shard_map/all_gather | solution.py:28
  8.0 159.4 %all-gather.5.cloned.1.call-start = ((), (), s32[]{:S(2)}) async-start(), calls=%async_computation.4 | async-start | bytes 1622016 | tf_op jit(solution)/shard_map/all_gather | solution.py:28
  8.8 251.0 %all-reduce.3.cloned.1.call-start = ((), (), s32[]{:S(2)}) async-start(), calls=%async_computation.6 | async-start | bytes 12582912 | tf_op jit(solution)/shard_map/psum | solution.py:32
  174.6 0.7 copy-start
  174.6 0.7 copy-start.2
  174.6 316.8 %reduce-scatter.3.cloned.1.call-start = ((), (), s32[]{:S(2)}) async-start(), calls=%async_computation.2 | async-start | bytes 3244032 | tf_op jit(solution)/shard_map/reduce_scatter | solution.py:34
  270.1 443.2 %reduce-scatter.5.cloned.1.call-start = ((), (), s32[]{:S(2)}) async-start(), calls=%async_computation.3 | async-start | bytes 3244032 | tf_op jit(solution)/shard_map/reduce_scatter | solution.py:34
  276.7 0.7 copy-start.1
Sparse Core Ops, SparseCore 0:
  9.9 80.1 all-gather.6
  92.7 74.6 all-gather.4
  174.7 85.0 all-reduce.2
  270.2 221.1 reduce-scatter.2
  495.6 217.6 reduce-scatter.4
where the time goes:
time: 722 us; the launch traced here: 721 us
  waiting for transfers between devices  672 us (93%)
  matrix products  28 us (4%)
  between operations  13.2 us (2%)
    reduce_scatter x2, waiting for transfers between devices, local(): lax.psum_scatter(jnp.dot(hidden, down_weight, preferred_element_type=jnp....  436 us
    all_gather x2, waiting for transfers between devices, local(): lax.all_gather(local_rows, 'dp', axis=0, tiled=True)  151 us
    psum x1, waiting for transfers between devices, local(): summed = lax.psum(partial_up, 'tensor')  84 us
  transfers between devices with their start and end apart: 5, of which 5 were waited for; matrix products, arithmetic and copies ran while one was open for 2% of the time, Pallas kernels for 0%

commit v1 on v0

v1 whole, which is shorter than its diff:
```python
import jax
import jax.numpy as jnp
from jax import lax
from jax.sharding import PartitionSpec as P

AXES = ("dp", "tensor")
NZ, NY, NX, NC = 8, 4, 4, 2
F32 = jnp.float32
BF16 = jnp.bfloat16


def shift(value, dz=0, dy=0, dx=0, dc=0):
    pairs = []
    for z in range(NZ):
        for y in range(NY):
            for x in range(NX):
                for c in range(NC):
                    source = ((z * NY + y) * NX + x) * NC + c
                    zt, yt, xt, ct = (z + dz) % NZ, (y + dy) % NY, (x + dx) % NX, (c + dc) % NC
                    pairs.append((source, ((zt * NY + yt) * NX + xt) * NC + ct))
    return lax.ppermute(value, AXES, pairs)


Z_SLOTS = (0, 1, -1, 2, -2, 3, 4, -3)
Y_SLOTS = (0, 1, -1, 2)


def gather_z(block):
    p1, m1 = shift(block, dz=1), shift(block, dz=-1)
    p2, m2 = shift(block, dz=2), shift(block, dz=-2)
    far = shift(jnp.concatenate([p1, p2]), dz=2)
    back = shift(m1, dz=-2)
    return jnp.concatenate([block, p1, m1, p2, m2, far, back])


def scatter_z(sums):
    far = shift(sums[5:7].astype(BF16), dz=-2).astype(F32)
    back = shift(sums[7:8].astype(BF16), dz=2).astype(F32)
    p1 = (sums[1] + far[0]).astype(BF16)
    p2 = (sums[3] + far[1]).astype(BF16)
    m1 = (sums[2] + back[0]).astype(BF16)
    m2 = sums[4].astype(BF16)
    return (
        sums[0]
        + shift(p1, dz=-1).astype(F32)
        + shift(m1, dz=1).astype(F32)
        + shift(p2, dz=-2).astype(F32)
        + shift(m2, dz=2).astype(F32)
    )


def local(tokens, up_weight, up_bias, down_weight, down_bias, active):
    steps, rows, width = tokens.shape
    hidden_width = up_weight.shape[1]
    blocks = active.shape[2]
    z = lax.axis_index("dp") // NY
    x = lax.axis_index("tensor") // NC
    c = lax.axis_index("tensor") % NC
    own = steps * rows
    slot = NZ * own
    half = NY * slot // NC
    piece = half // NX

    column = gather_z(tokens.reshape(own, width))
    gathered = jnp.concatenate([column] + [shift(column, dy=k) for k in Y_SLOTS[1:]])

    def project(start):
        part = lax.dynamic_slice_in_dim(gathered, start, half)
        return jnp.dot(part, up_weight, preferred_element_type=F32)

    away = shift(project((1 - c) * half).astype(BF16), dc=1)
    sums = project(c * half) + away.astype(F32)

    def piece_for(k):
        return lax.dynamic_slice_in_dim(sums, ((x + k) % NX) * piece, piece)

    total = piece_for(0)
    for k in (1, -1, 2):
        total = total + shift(piece_for(k).astype(BF16), dx=k).astype(F32)

    z_slots = jnp.asarray(Z_SLOTS, jnp.int32).reshape(2, 4)[x % 2]
    row_block = ((z - z_slots) % NZ) // 2
    mask = jnp.swapaxes(jnp.take(active, row_block, axis=1), 0, 1)
    mask = mask.astype(F32)[:, :, None, :, None]
    preact = jnp.maximum(total + up_bias.astype(F32), 0.0)
    gated = preact.reshape(4, steps, rows, blocks, hidden_width // blocks) * mask
    mine = gated.reshape(piece, hidden_width).astype(BF16)

    near = jnp.zeros((half, hidden_width), BF16)
    near = lax.dynamic_update_slice_in_dim(near, mine, x * piece, 0)
    for k in (1, -1, 2):
        near = lax.dynamic_update_slice_in_dim(near, shift(mine, dx=k), ((x - k) % NX) * piece, 0)
    other = shift(near, dc=1)
    hidden = jnp.concatenate([jnp.where(c == 0, near, other), jnp.where(c == 0, other, near)])

    outs = [
        jnp.dot(hidden[i * slot : (i + 1) * slot], down_weight, preferred_element_type=F32)
        for i in range(NY)
    ]
    scattered = outs[0]
    for i in (1, 2, 3):
        scattered = scattered + shift(outs[i].astype(BF16), dy=-Y_SLOTS[i]).astype(F32)
    mixed = scatter_z(scattered.reshape(NZ, own, width)) + down_bias.astype(F32)
    return mixed.astype(BF16).reshape(steps, rows, width)


def solution(mesh):
    placed = (
        P(None, "dp", "tensor"),
        P("tensor", "dp"),
        P("dp"),
        P("dp", "tensor"),
        P("tensor"),
        P(None, None, "dp"),
    )
    return jax.shard_map(
        local, mesh=mesh, in_specs=placed, out_specs=P(None, "dp", "tensor"), check_vma=False
    )
```

time: 722 us -> 196 us (0.27)
  waiting for transfers between devices: 672 us -> 122 us
  starting transfers between devices: 0.17 us -> 41.3 us
  between operations: 13.2 us -> 0.26 us
  matrix products: 28 us -> 18.3 us
  local copies, waits for them, and re-layouts: 2.74 us -> 11.1 us
    reduce_scatter x2 -> x0, waiting for transfers between devices: 436 us -> none  [local(): lax.psum_scatter(jnp.dot(hidden, down_weight, preferred_element_type=jnp....]
    all_gather x2 -> x0, waiting for transfers between devices: 151 us -> none  [local(): lax.all_gather(local_rows, 'dp', axis=0, tiled=True)]
    ppermute x0 -> x26, waiting for transfers between devices: none -> 122 us  [shift(): return lax.ppermute(value, AXES, pairs)]
    psum x1 -> x0, waiting for transfers between devices: 84 us -> none  [local(): summed = lax.psum(partial_up, 'tensor')]
    ppermute x0 -> x26, starting transfers between devices: none -> 41.3 us  [shift(): return lax.ppermute(value, AXES, pairs)]
    dot_general x6, matrix products: 28 us -> 18.3 us  [the longest x2 10.1 us: project(): return jnp.dot(part, up_weight, preferred_element_type=F32)]
  transfers between devices with their start and end apart: 5 -> 26, of which waited for: 5 -> 18; matrix products, arithmetic and copies ran while one was open for 2% -> 4% of each run, Pallas kernels for 0% -> 0%
where the time goes in v1:
time: 196 us
  waiting for transfers between devices  122 us (62%)
  starting transfers between devices  41.3 us (21%)
  matrix products  18.3 us (9%)
  local copies, waits for them, and re-layouts  11.1 us (6%)
  other arithmetic  2.82 us (1%)
    ppermute x26, waiting for transfers between devices, shift(): return lax.ppermute(value, AXES, pairs)  122 us
    ppermute x26, starting transfers between devices, shift(): return lax.ppermute(value, AXES, pairs)  41.3 us
    dot_general x2, matrix products, project(): return jnp.dot(part, up_weight, preferred_element_type=F32)  10.1 us
    unnamed x24, local copies, waits for them, and re-layouts  8.45 us
    dot_general x4, matrix products, local(): jnp.dot(hidden[i * slot:(i + 1) * slot], down_weight, preferred_element_t...  8.21 us
  transfers between devices with their start and end apart: 26, of which 18 were waited for; matrix products, arithmetic and copies ran while one was open for 4% of the time, Pallas kernels for 0%

profile of v1, /device:TPU:6, one launch (start us, length us, event | category | flops | bytes accessed | tf_op | source)
XLA Modules:
  0.0 196.2 jit_solution(165090188086833264)
XLA Ops:
  1.9 4.0 %collective-permute-start.1 = (bf16[32,1536]{1,0:T(8,128)(2,1)}, bf16[32,1536]{1,0:T(8,128)(2,1)S(1)}, u32[]{:S(2)}, u32[]{:S(2)}) collective-permute-start(bf16[32,1536]{1,0:T(8,128)(2,1)} %bitcast.50), channel_id=1, source_target_pairs={{0,224},{1,225},{2,226},{3,227},{4,228},{5,229},{6,230},{7,231},{8... | collective-permute-start | bytes 294920 | tf_op jit(solution)/shard_map/ppermute | solution.py:21
  5.9 4.1 %collective-permute-start.3 = (bf16[32,1536]{1,0:T(8,128)(2,1)}, bf16[32,1536]{1,0:T(8,128)(2,1)S(1)}, u32[]{:S(2)}, u32[]{:S(2)}) collective-permute-start(bf16[32,1536]{1,0:T(8,128)(2,1)} %bitcast.52), channel_id=1, source_target_pairs={{0,192},{1,193},{2,194},{3,195},{4,196},{5,197},{6,198},{7,199},{8... | collective-permute-start | bytes 294920 | tf_op jit(solution)/shard_map/ppermute | solution.py:21
  11.7 2.8 %collective-permute-done.2 = bf16[32,1536]{1,0:T(8,128)(2,1)S(1)} collective-permute-done((bf16[32,1536]{1,0:T(8,128)(2,1)}, bf16[32,1536]{1,0:T(8,128)(2,1)S(1)}, u32[]{:S(2)}, u32[]{:S(2)}) %collective-permute-start.2) | collective-permute-done | bytes 98336 | tf_op jit(solution)/shard_map/ppermute | solution.py:21
  14.6 4.1 %collective-permute-start.5 = (bf16[32,1536]{1,0:T(8,128)(2,1)S(1)}, bf16[32,1536]{1,0:T(8,128)(2,1)S(1)}, u32[]{:S(2)}, u32[]{:S(2)}) collective-permute-start(bf16[32,1536]{1,0:T(8,128)(2,1)S(1)} %collective-permute-done.1), channel_id=1, source_target_pairs={{0,192},{1,193},{2,194},{3,195},{4,196},{5,197},{6,198},{7,199},{8... | collective-permute-start | bytes 294920 | tf_op jit(solution)/shard_map/ppermute | solution.py:21
  21.3 3.5 %collective-permute-done.4 = bf16[64,1536]{1,0:T(8,128)(2,1)S(1)} collective-permute-done((bf16[64,1536]{1,0:T(8,128)(2,1)S(1)}, bf16[64,1536]{1,0:T(8,128)(2,1)S(1)}, u32[]{:S(2)}, u32[]{:S(2)}) %collective-permute-start.4) | collective-permute-done | bytes 196640 | tf_op jit(solution)/shard_map/ppermute | solution.py:21
  31.5 15.3 %collective-permute-done.6 = bf16[256,1536]{1,0:T(8,128)(2,1)S(1)} collective-permute-done((bf16[256,1536]{1,0:T(8,128)(2,1)S(1)}, bf16[256,1536]{1,0:T(8,128)(2,1)S(1)}, u32[]{:S(2)}, u32[]{:S(2)}) %collective-permute-start.6) | collective-permute-done | bytes 786464 | tf_op jit(solution)/shard_map/ppermute | solution.py:21
  49.3 14.8 %collective-permute-done.8 = bf16[256,1536]{1,0:T(8,128)(2,1)S(1)} collective-permute-done((bf16[256,1536]{1,0:T(8,128)(2,1)S(1)}, bf16[256,1536]{1,0:T(8,128)(2,1)S(1)}, u32[]{:S(2)}, u32[]{:S(2)}) %collective-permute-start.8) | collective-permute-done | bytes 786464 | tf_op jit(solution)/shard_map/ppermute | solution.py:21
  65.0 5.1 %convolution_convert_fusion = bf16[512,1536]{1,0:T(8,128)(2,1)} fusion(bf16[1536,1536]{1,0:T(8,128)(2,1)S(1)} %copy-done.5, bf16[1024,1536]{1,0:T(8,128)(2,1)} %constant_dynamic-update-slice_fusion.7, s32[]{:T(128)S(6)} %select_n.140), kind=kOutput, calls=%fused_computation.2 | convolution fusion | flops 2416705536 | bytes 7864324 | tf_op jit(solution)/shard_map/dot_general | solution.py:69
  70.2 3.6 %collective-permute-done.9 = bf16[512,1536]{1,0:T(8,128)(2,1)S(1)} collective-permute-done((bf16[512,1536]{1,0:T(8,128)(2,1)}, bf16[512,1536]{1,0:T(8,128)(2,1)S(1)}, u32[]{:S(2)}, u32[]{:S(2)}) %collective-permute-start.9) | collective-permute-done | bytes 1572896 | tf_op jit(solution)/shard_map/ppermute | solution.py:21
  73.8 4.9 %convolution_add_fusion = f32[512,1536]{1,0:T(8,128)S(1)} fusion(bf16[1536,1536]{1,0:T(8,128)(2,1)} %param.8, bf16[512,1536]{1,0:T(8,128)(2,1)S(1)} %collective-permute-done.9, bf16[1024,1536]{1,0:T(8,128)(2,1)} %constant_dynamic-update-slice_fusion.7, s32[]{:T(128)S(6)} %select_n.139), kind=kOutput, calls=%fused_computation.1 | convolution fusion | flops 2417491968 | bytes 11010052 | tf_op jit(solution)/shard_map/dot_general | solution.py:69
  84.7 7.8 %collective-permute-done.10 = bf16[128,1536]{1,0:T(8,128)(2,1)S(1)} collective-permute-done((bf16[128,1536]{1,0:T(8,128)(2,1)S(1)}, bf16[128,1536]{1,0:T(8,128)(2,1)S(1)}, u32[]{:S(2)}, u32[]{:S(2)}) %collective-permute-start.10) | collective-permute-done | bytes 393248 | tf_op jit(solution)/shard_map/ppermute | solution.py:21
  92.5 9.0 %collective-permute-done.11 = bf16[128,1536]{1,0:T(8,128)(2,1)S(1)} collective-permute-done((bf16[128,1536]{1,0:T(8,128)(2,1)S(1)}, bf16[128,1536]{1,0:T(8,128)(2,1)S(1)}, u32[]{:S(2)}, u32[]{:S(2)}) %collective-permute-start.11) | collective-permute-done | bytes 393248 | tf_op jit(solution)/shard_map/ppermute | solution.py:21
  107.4 13.7 %collective-permute-done.13 = bf16[128,1536]{1,0:T(8,128)(2,1)S(1)} collective-permute-done((bf16[128,1536]{1,0:T(8,128)(2,1)S(1)}, bf16[128,1536]{1,0:T(8,128)(2,1)S(1)}, u32[]{:S(2)}, u32[]{:S(2)}) %collective-permute-start.13) | collective-permute-done | bytes 393248 | tf_op jit(solution)/shard_map/ppermute | solution.py:21
  121.1 3.3 %collective-permute-done.14 = bf16[128,1536]{1,0:T(8,128)(2,1)S(1)} collective-permute-done((bf16[128,1536]{1,0:T(8,128)(2,1)S(1)}, bf16[128,1536]{1,0:T(8,128)(2,1)S(1)}, u32[]{:S(2)}, u32[]{:S(2)}) %collective-permute-start.14) | collective-permute-done | bytes 393248 | tf_op jit(solution)/shard_map/ppermute | solution.py:21
  124.7 3.4 %collective-permute-done.16 = bf16[512,1536]{1,0:T(8,128)(2,1)S(1)} collective-permute-done((bf16[512,1536]{1,0:T(8,128)(2,1)S(1)}, bf16[512,1536]{1,0:T(8,128)(2,1)S(1)}, u32[]{:S(2)}, u32[]{:S(2)}) %collective-permute-start.16) | collective-permute-done | bytes 1572896 | tf_op jit(solution)/shard_map/ppermute | solution.py:21
  128.3 3.9 %convolution_convert_fusion.2 = bf16[256,1536]{1,0:T(8,128)(2,1)S(1)} fusion(bf16[1536,1536]{1,0:T(8,128)(2,1)} %param.10, bf16[512,1536]{1,0:T(8,128)(2,1)S(1)} %get-tuple-element.8), kind=kOutput, calls=%fused_computation.7 | convolution fusion | flops 1208352768 | bytes 6291456 | tf_op jit(solution)/shard_map/dot_general | solution.py:97
  135.0 2.8 %collective-permute-start.17 = (bf16[256,1536]{1,0:T(8,128)(2,1)S(1)}, bf16[256,1536]{1,0:T(8,128)(2,1)S(1)}, u32[]{:S(2)}, u32[]{:S(2)}) collective-permute-start(bf16[256,1536]{1,0:T(8,128)(2,1)S(1)} %convolution_convert_fusion.3), channel_id=1, source_target_pairs={{0,24},{1,25},{2,26},{3,27},{4,28},{5,29},{6,30},{7,31},{8,0},{9,1... | collective-permute-start | bytes 2359304 | tf_op jit(solution)/shard_map/ppermute | solution.py:21
  139.7 32.0 %collective-permute-done.17 = bf16[256,1536]{1,0:T(8,128)(2,1)S(1)} collective-permute-done((bf16[256,1536]{1,0:T(8,128)(2,1)S(1)}, bf16[256,1536]{1,0:T(8,128)(2,1)S(1)}, u32[]{:S(2)}, u32[]{:S(2)}) %collective-permute-start.17) | collective-permute-done | bytes 786464 | tf_op jit(solution)/shard_map/ppermute | solution.py:21
  171.8 3.4 %collective-permute-done.18 = bf16[256,1536]{1,0:T(8,128)(2,1)S(1)} collective-permute-done((bf16[256,1536]{1,0:T(8,128)(2,1)S(1)}, bf16[256,1536]{1,0:T(8,128)(2,1)S(1)}, u32[]{:S(2)}, u32[]{:S(2)}) %collective-permute-start.18) | collective-permute-done | bytes 786464 | tf_op jit(solution)/shard_map/ppermute | solution.py:21
  176.8 3.6 %collective-permute-start.20 = (bf16[2,32,1536]{2,1,0:T(8,128)(2,1)S(1)}, bf16[2,32,1536]{2,1,0:T(8,128)(2,1)S(1)}, u32[]{:S(2)}, u32[]{:S(2)}) collective-permute-start(bf16[2,32,1536]{2,1,0:T(8,128)(2,1)S(1)} %bitcast.48), channel_id=1, source_target_pairs={{0,192},{1,193},{2,194},{3,195},{4,196},{5,197},{6,198},{7,199},{8... | collective-permute-start | bytes 589832 | tf_op jit(solution)/shard_map/ppermute | solution.py:21
  180.4 2.6 %collective-permute-start.25 = (bf16[32,1536]{1,0:T(8,128)(2,1)S(1)}, bf16[32,1536]{1,0:T(8,128)(2,1)S(1)}, u32[]{:S(2)}, u32[]{:S(2)}) collective-permute-start(bf16[32,1536]{1,0:T(8,128)(2,1)S(1)} %get-tuple-element.16), channel_id=1, source_target_pairs={{0,64},{1,65},{2,66},{3,67},{4,68},{5,69},{6,70},{7,71},{8,72},{9,... | collective-permute-start | bytes 294920 | tf_op jit(solution)/shard_map/ppermute | solution.py:21
  183.7 3.5 %collective-permute-done.22 = bf16[1,32,1536]{2,1,0:T(8,128)(2,1)S(1)} collective-permute-done((bf16[1,32,1536]{2,1,0:T(8,128)(2,1)S(1)}, bf16[1,32,1536]{2,1,0:T(8,128)(2,1)S(1)}, u32[]{:S(2)}, u32[]{:S(2)}) %collective-permute-start.22) | collective-permute-done | bytes 98336 | tf_op jit(solution)/shard_map/ppermute | solution.py:21
  190.5 2.6 %collective-permute-done.21 = bf16[32,1536]{1,0:T(8,128)(2,1)S(1)} collective-permute-done((bf16[32,1536]{1,0:T(8,128)(2,1)S(1)}, bf16[32,1536]{1,0:T(8,128)(2,1)S(1)}, u32[]{:S(2)}, u32[]{:S(2)}) %collective-permute-start.21) | collective-permute-done | bytes 98336 | tf_op jit(solution)/shard_map/ppermute | solution.py:21
  193.2 2.2 %collective-permute-done.24 = bf16[32,1536]{1,0:T(8,128)(2,1)S(1)} collective-permute-done((bf16[32,1536]{1,0:T(8,128)(2,1)S(1)}, bf16[32,1536]{1,0:T(8,128)(2,1)S(1)}, u32[]{:S(2)}, u32[]{:S(2)}) %collective-permute-start.24) | collective-permute-done | bytes 98336 | tf_op jit(solution)/shard_map/ppermute | solution.py:21
  (83 shorter events, 39.5 us)
Async XLA Ops:
  0.0 11.7 %collective-permute-start = (bf16[32,1536]{1,0:T(8,128)(2,1)}, bf16[32,1536]{1,0:T(8,128)(2,1)S(1)}, u32[]{:S(2)}, u32[]{:S(2)}) collective-permute-start(bf16[32,1536]{1,0:T(8,128)(2,1)} %bitcast.49), channel_id=1, source_target_pairs={{0,32},{1,33},{2,34},{3,35},{4,36},{5,37},{6,38},{7,39},{8,40},{9,... | collective-permute-start | bytes 294920 | tf_op jit(solution)/shard_map/ppermute | solution.py:21
  1.9 12.7 %collective-permute-start.1 = (bf16[32,1536]{1,0:T(8,128)(2,1)}, bf16[32,1536]{1,0:T(8,128)(2,1)S(1)}, u32[]{:S(2)}, u32[]{:S(2)}) collective-permute-start(bf16[32,1536]{1,0:T(8,128)(2,1)} %bitcast.50), channel_id=1, source_target_pairs={{0,224},{1,225},{2,226},{3,227},{4,228},{5,229},{6,230},{7,231},{8... | collective-permute-start | bytes 294920 | tf_op jit(solution)/shard_map/ppermute | solution.py:21
  5.9 8.6 %collective-permute-start.2 = (bf16[32,1536]{1,0:T(8,128)(2,1)}, bf16[32,1536]{1,0:T(8,128)(2,1)S(1)}, u32[]{:S(2)}, u32[]{:S(2)}) collective-permute-start(bf16[32,1536]{1,0:T(8,128)(2,1)} %bitcast.51), channel_id=1, source_target_pairs={{0,64},{1,65},{2,66},{3,67},{4,68},{5,69},{6,70},{7,71},{8,72},{9,... | collective-permute-start | bytes 294920 | tf_op jit(solution)/shard_map/ppermute | solution.py:21
  5.9 14.7 %collective-permute-start.3 = (bf16[32,1536]{1,0:T(8,128)(2,1)}, bf16[32,1536]{1,0:T(8,128)(2,1)S(1)}, u32[]{:S(2)}, u32[]{:S(2)}) collective-permute-start(bf16[32,1536]{1,0:T(8,128)(2,1)} %bitcast.52), channel_id=1, source_target_pairs={{0,192},{1,193},{2,194},{3,195},{4,196},{5,197},{6,198},{7,199},{8... | collective-permute-start | bytes 294920 | tf_op jit(solution)/shard_map/ppermute | solution.py:21
  14.5 10.4 %collective-permute-start.4 = (bf16[64,1536]{1,0:T(8,128)(2,1)S(1)}, bf16[64,1536]{1,0:T(8,128)(2,1)S(1)}, u32[]{:S(2)}, u32[]{:S(2)}) collective-permute-start(bf16[64,1536]{1,0:T(8,128)(2,1)S(1)} %pad_maximum_fusion), channel_id=1, source_target_pairs={{0,64},{1,65},{2,66},{3,67},{4,68},{5,69},{6,70},{7,71},{8,72},{9,... | collective-permute-start | bytes 589832 | tf_op jit(solution)/shard_map/ppermute | solution.py:21
  14.6 11.0 %collective-permute-start.5 = (bf16[32,1536]{1,0:T(8,128)(2,1)S(1)}, bf16[32,1536]{1,0:T(8,128)(2,1)S(1)}, u32[]{:S(2)}, u32[]{:S(2)}) collective-permute-start(bf16[32,1536]{1,0:T(8,128)(2,1)S(1)} %collective-permute-done.1), channel_id=1, source_target_pairs={{0,192},{1,193},{2,194},{3,195},{4,196},{5,197},{6,198},{7,199},{8... | collective-permute-start | bytes 294920 | tf_op jit(solution)/shard_map/ppermute | solution.py:21
  26.3 20.6 %collective-permute-start.6 = (bf16[256,1536]{1,0:T(8,128)(2,1)S(1)}, bf16[256,1536]{1,0:T(8,128)(2,1)S(1)}, u32[]{:S(2)}, u32[]{:S(2)}) collective-permute-start(bf16[256,1536]{1,0:T(8,128)(2,1)S(1)} %get-tuple-element.19), channel_id=1, source_target_pairs={{0,8},{1,9},{2,10},{3,11},{4,12},{5,13},{6,14},{7,15},{8,16},{9,17... | collective-permute-start | bytes 2359304 | tf_op jit(solution)/shard_map/ppermute | solution.py:21
  27.8 20.5 %collective-permute-start.7 = (bf16[256,1536]{1,0:T(8,128)(2,1)S(1)}, bf16[256,1536]{1,0:T(8,128)(2,1)S(1)}, u32[]{:S(2)}, u32[]{:S(2)}) collective-permute-start(bf16[256,1536]{1,0:T(8,128)(2,1)S(1)} %get-tuple-element.19), channel_id=1, source_target_pairs={{0,24},{1,25},{2,26},{3,27},{4,28},{5,29},{6,30},{7,31},{8,0},{9,1... | collective-permute-start | bytes 2359304 | tf_op jit(solution)/shard_map/ppermute | solution.py:21
  29.5 34.6 %collective-permute-start.8 = (bf16[256,1536]{1,0:T(8,128)(2,1)S(1)}, bf16[256,1536]{1,0:T(8,128)(2,1)S(1)}, u32[]{:S(2)}, u32[]{:S(2)}) collective-permute-start(bf16[256,1536]{1,0:T(8,128)(2,1)S(1)} %get-tuple-element.19), channel_id=1, source_target_pairs={{0,16},{1,17},{2,18},{3,19},{4,20},{5,21},{6,22},{7,23},{8,24},{9,... | collective-permute-start | bytes 2359304 | tf_op jit(solution)/shard_map/ppermute | solution.py:21
  80.5 12.0 %collective-permute-start.10 = (bf16[128,1536]{1,0:T(8,128)(2,1)S(1)}, bf16[128,1536]{1,0:T(8,128)(2,1)S(1)}, u32[]{:S(2)}, u32[]{:S(2)}) collective-permute-start(bf16[128,1536]{1,0:T(8,128)(2,1)S(1)} %get-tuple-element.9), channel_id=1, source_target_pairs={{0,2},{1,3},{2,4},{3,5},{4,6},{5,7},{6,0},{7,1},{8,10},{9,11},{10,... | collective-permute-start | bytes 1179656 | tf_op jit(solution)/shard_map/ppermute | solution.py:21
  81.0 20.5 %collective-permute-start.11 = (bf16[128,1536]{1,0:T(8,128)(2,1)S(1)}, bf16[128,1536]{1,0:T(8,128)(2,1)S(1)}, u32[]{:S(2)}, u32[]{:S(2)}) collective-permute-start(bf16[128,1536]{1,0:T(8,128)(2,1)S(1)} %get-tuple-element.11), channel_id=1, source_target_pairs={{0,6},{1,7},{2,0},{3,1},{4,2},{5,3},{6,4},{7,5},{8,14},{9,15},{10,... | collective-permute-start | bytes 1179656 | tf_op jit(solution)/shard_map/ppermute | solution.py:21
  82.6 19.0 %collective-permute-start.12 = (bf16[128,1536]{1,0:T(8,128)(2,1)S(1)}, bf16[128,1536]{1,0:T(8,128)(2,1)S(1)}, u32[]{:S(2)}, u32[]{:S(2)}) collective-permute-start(bf16[128,1536]{1,0:T(8,128)(2,1)S(1)} %get-tuple-element.10), channel_id=1, source_target_pairs={{0,4},{1,5},{2,6},{3,7},{4,0},{5,1},{6,2},{7,3},{8,12},{9,13},{10,... | collective-permute-start | bytes 1179656 | tf_op jit(solution)/shard_map/ppermute | solution.py:21
  103.5 17.6 %collective-permute-start.13 = (bf16[128,1536]{1,0:T(8,128)(2,1)S(1)}, bf16[128,1536]{1,0:T(8,128)(2,1)S(1)}, u32[]{:S(2)}, u32[]{:S(2)}) collective-permute-start(bf16[128,1536]{1,0:T(8,128)(2,1)S(1)} %get-tuple-element.6), channel_id=1, source_target_pairs={{0,2},{1,3},{2,4},{3,5},{4,6},{5,7},{6,0},{7,1},{8,10},{9,11},{10,... | collective-permute-start | bytes 1179656 | tf_op jit(solution)/shard_map/ppermute | solution.py:21
  104.8 19.7 %collective-permute-start.14 = (bf16[128,1536]{1,0:T(8,128)(2,1)S(1)}, bf16[128,1536]{1,0:T(8,128)(2,1)S(1)}, u32[]{:S(2)}, u32[]{:S(2)}) collective-permute-start(bf16[128,1536]{1,0:T(8,128)(2,1)S(1)} %get-tuple-element.6), channel_id=1, source_target_pairs={{0,6},{1,7},{2,0},{3,1},{4,2},{5,3},{6,4},{7,5},{8,14},{9,15},{10,... | collective-permute-start | bytes 1179656 | tf_op jit(solution)/shard_map/ppermute | solution.py:21
  105.6 19.0 %collective-permute-start.15 = (bf16[128,1536]{1,0:T(8,128)(2,1)S(1)}, bf16[128,1536]{1,0:T(8,128)(2,1)S(1)}, u32[]{:S(2)}, u32[]{:S(2)}) collective-permute-start(bf16[128,1536]{1,0:T(8,128)(2,1)S(1)} %get-tuple-element.6), channel_id=1, source_target_pairs={{0,4},{1,5},{2,6},{3,7},{4,0},{5,1},{6,2},{7,3},{8,12},{9,13},{10,... | collective-permute-start | bytes 1179656 | tf_op jit(solution)/shard_map/ppermute | solution.py:21
  135.0 36.8 %collective-permute-start.17 = (bf16[256,1536]{1,0:T(8,128)(2,1)S(1)}, bf16[256,1536]{1,0:T(8,128)(2,1)S(1)}, u32[]{:S(2)}, u32[]{:S(2)}) collective-permute-start(bf16[256,1536]{1,0:T(8,128)(2,1)S(1)} %convolution_convert_fusion.3), channel_id=1, source_target_pairs={{0,24},{1,25},{2,26},{3,27},{4,28},{5,29},{6,30},{7,31},{8,0},{9,1... | collective-permute-start | bytes 2359304 | tf_op jit(solution)/shard_map/ppermute | solution.py:21
  137.8 37.4 %collective-permute-start.18 = (bf16[256,1536]{1,0:T(8,128)(2,1)S(1)}, bf16[256,1536]{1,0:T(8,128)(2,1)S(1)}, u32[]{:S(2)}, u32[]{:S(2)}) collective-permute-start(bf16[256,1536]{1,0:T(8,128)(2,1)S(1)} %convolution_convert_fusion.2), channel_id=1, source_target_pairs={{0,8},{1,9},{2,10},{3,11},{4,12},{5,13},{6,14},{7,15},{8,16},{9,17... | collective-permute-start | bytes 2359304 | tf_op jit(solution)/shard_map/ppermute | solution.py:21
  137.8 37.4 %collective-permute-start.19 = (bf16[256,1536]{1,0:T(8,128)(2,1)S(1)}, bf16[256,1536]{1,0:T(8,128)(2,1)S(1)}, u32[]{:S(2)}, u32[]{:S(2)}) collective-permute-start(bf16[256,1536]{1,0:T(8,128)(2,1)S(1)} %convolution_convert_fusion.1), channel_id=1, source_target_pairs={{0,16},{1,17},{2,18},{3,19},{4,20},{5,21},{6,22},{7,23},{8,24},{9,... | collective-permute-start | bytes 2359304 | tf_op jit(solution)/shard_map/ppermute | solution.py:21
  176.8 6.9 %collective-permute-start.20 = (bf16[2,32,1536]{2,1,0:T(8,128)(2,1)S(1)}, bf16[2,32,1536]{2,1,0:T(8,128)(2,1)S(1)}, u32[]{:S(2)}, u32[]{:S(2)}) collective-permute-start(bf16[2,32,1536]{2,1,0:T(8,128)(2,1)S(1)} %bitcast.48), channel_id=1, source_target_pairs={{0,192},{1,193},{2,194},{3,195},{4,196},{5,197},{6,198},{7,199},{8... | collective-permute-start | bytes 589832 | tf_op jit(solution)/shard_map/ppermute | solution.py:21
  180.4 6.8 %collective-permute-start.22 = (bf16[1,32,1536]{2,1,0:T(8,128)(2,1)S(1)}, bf16[1,32,1536]{2,1,0:T(8,128)(2,1)S(1)}, u32[]{:S(2)}, u32[]{:S(2)}) collective-permute-start(bf16[1,32,1536]{2,1,0:T(8,128)(2,1)S(1)} %get-tuple-element.15), channel_id=1, source_target_pairs={{0,64},{1,65},{2,66},{3,67},{4,68},{5,69},{6,70},{7,71},{8,72},{9,... | collective-permute-start | bytes 294920 | tf_op jit(solution)/shard_map/ppermute | solution.py:21
  180.4 10.0 %collective-permute-start.25 = (bf16[32,1536]{1,0:T(8,128)(2,1)S(1)}, bf16[32,1536]{1,0:T(8,128)(2,1)S(1)}, u32[]{:S(2)}, u32[]{:S(2)}) collective-permute-start(bf16[32,1536]{1,0:T(8,128)(2,1)S(1)} %get-tuple-element.16), channel_id=1, source_target_pairs={{0,64},{1,65},{2,66},{3,67},{4,68},{5,69},{6,70},{7,71},{8,72},{9,... | collective-permute-start | bytes 294920 | tf_op jit(solution)/shard_map/ppermute | solution.py:21
  187.2 5.9 %collective-permute-start.21 = (bf16[32,1536]{1,0:T(8,128)(2,1)S(1)}, bf16[32,1536]{1,0:T(8,128)(2,1)S(1)}, u32[]{:S(2)}, u32[]{:S(2)}) collective-permute-start(bf16[32,1536]{1,0:T(8,128)(2,1)S(1)} %get-tuple-element.12), channel_id=1, source_target_pairs={{0,224},{1,225},{2,226},{3,227},{4,228},{5,229},{6,230},{7,231},{8... | collective-permute-start | bytes 294920 | tf_op jit(solution)/shard_map/ppermute | solution.py:21
  187.3 5.9 %collective-permute-start.23 = (bf16[32,1536]{1,0:T(8,128)(2,1)S(1)}, bf16[32,1536]{1,0:T(8,128)(2,1)S(1)}, u32[]{:S(2)}, u32[]{:S(2)}) collective-permute-start(bf16[32,1536]{1,0:T(8,128)(2,1)S(1)} %get-tuple-element.14), channel_id=1, source_target_pairs={{0,32},{1,33},{2,34},{3,35},{4,36},{5,37},{6,38},{7,39},{8,40},{9,... | collective-permute-start | bytes 294920 | tf_op jit(solution)/shard_map/ppermute | solution.py:21
  189.3 6.1 %collective-permute-start.24 = (bf16[32,1536]{1,0:T(8,128)(2,1)S(1)}, bf16[32,1536]{1,0:T(8,128)(2,1)S(1)}, u32[]{:S(2)}, u32[]{:S(2)}) collective-permute-start(bf16[32,1536]{1,0:T(8,128)(2,1)S(1)} %get-tuple-element.13), channel_id=1, source_target_pairs={{0,192},{1,193},{2,194},{3,195},{4,196},{5,197},{6,198},{7,199},{8... | collective-permute-start | bytes 294920 | tf_op jit(solution)/shard_map/ppermute | solution.py:21
  (10 other events, 209.5 us)

commit v2 on v0

v2 whole, which is shorter than its diff:
```python
import jax
import jax.numpy as jnp
from jax import lax
from jax.experimental import pallas as pl
from jax.experimental.pallas import tpu as pltpu
from jax.sharding import PartitionSpec as P

AXES = ("dp", "tensor")
NZ, NY, NX, NC = 8, 4, 4, 2
Z_GROUPS = [[z * NY + y for z in range(NZ)] for y in range(NY)]
F32 = jnp.float32
BF16 = jnp.bfloat16
TILE = 256
VMEM = pl.BlockSpec(memory_space=pltpu.VMEM)


def shift(value, dz=0, dy=0, dx=0, dc=0):
    pairs = []
    for z in range(NZ):
        for y in range(NY):
            for x in range(NX):
                for c in range(NC):
                    source = ((z * NY + y) * NX + x) * NC + c
                    zt, yt, xt, ct = (z + dz) % NZ, (y + dy) % NY, (x + dx) % NX, (c + dc) % NC
                    pairs.append((source, ((zt * NY + yt) * NX + xt) * NC + ct))
    return lax.ppermute(value, AXES, pairs)


def exchange_z(blocks):
    return lax.all_to_all(blocks, "dp", 0, 0, tiled=True, axis_index_groups=Z_GROUPS)


def gather_z(block):
    copies = jnp.broadcast_to(block[None], (NZ,) + block.shape)
    return exchange_z(copies).reshape(NZ * block.shape[0], block.shape[1])


def up_kernel(col, prev, succ, far, weight, own, away, held):
    c = lax.axis_index("tensor") % NC
    j = pl.program_id(0)
    slot = col.shape[0]
    half = own.shape[0]

    @pl.when(j == 0)
    def _():
        near_at = pl.multiple_of(c * half, half)
        far_at = pl.multiple_of((1 - c) * half, half)
        held[pl.ds(near_at, slot), :] = col[...]
        held[pl.ds(near_at + slot, slot), :] = prev[...]
        held[pl.ds(far_at, slot), :] = succ[...]
        held[pl.ds(far_at + slot, slot), :] = far[...]

    columns = pl.ds(pl.multiple_of(j * TILE, TILE), TILE)
    product = jnp.dot(held[...], weight[...], preferred_element_type=F32)
    own[:, columns] = product[:half]
    away[:, columns] = product[half:].astype(BF16)


def up(col, prev, succ, far, weight):
    slot, depth = col.shape
    width = weight.shape[1]
    half = 2 * slot
    return pl.pallas_call(
        up_kernel,
        grid=(width // TILE,),
        in_specs=[VMEM] * 4 + [pl.BlockSpec((depth, TILE), lambda j: (0, j))],
        out_specs=[VMEM] * 2,
        out_shape=[
            jax.ShapeDtypeStruct((half, width), F32),
            jax.ShapeDtypeStruct((half, width), BF16),
        ],
        scratch_shapes=[pltpu.VMEM((2 * half, depth), BF16)],
        compiler_params=pltpu.CompilerParams(vmem_limit_bytes=24 * 2**20),
        cost_estimate=pl.CostEstimate(
            flops=4 * half * depth * width, bytes_accessed=2 * depth * width, transcendentals=0
        ),
    )(col, prev, succ, far, weight)


def down_kernel(near, other, weight, out0, out1, out2, out3, held):
    c = lax.axis_index("tensor") % NC
    j = pl.program_id(0)
    half = near.shape[0]
    slot = out0.shape[0]

    @pl.when(j == 0)
    def _():
        held[pl.ds(pl.multiple_of(c * half, half), half), :] = near[...]
        held[pl.ds(pl.multiple_of((1 - c) * half, half), half), :] = other[...]

    columns = pl.ds(pl.multiple_of(j * TILE, TILE), TILE)
    product = jnp.dot(held[...], weight[...], preferred_element_type=F32)
    out0[:, columns] = product[:slot]
    out1[:, columns] = product[slot : 2 * slot].astype(BF16)
    out2[:, columns] = product[2 * slot : 3 * slot].astype(BF16)
    out3[:, columns] = product[3 * slot :].astype(BF16)


def down(near, other, weight):
    half, depth = near.shape
    width = weight.shape[1]
    slot = half // 2
    return pl.pallas_call(
        down_kernel,
        grid=(width // TILE,),
        in_specs=[VMEM] * 2 + [pl.BlockSpec((depth, TILE), lambda j: (0, j))],
        out_specs=[VMEM] * 4,
        out_shape=[jax.ShapeDtypeStruct((slot, width), F32)]
        + [jax.ShapeDtypeStruct((slot, width), BF16)] * 3,
        scratch_shapes=[pltpu.VMEM((2 * half, depth), BF16)],
        compiler_params=pltpu.CompilerParams(vmem_limit_bytes=24 * 2**20),
        cost_estimate=pl.CostEstimate(
            flops=4 * half * depth * width, bytes_accessed=2 * depth * width, transcendentals=0
        ),
    )(near, other, weight)


def local(tokens, up_weight, up_bias, down_weight, down_bias, active):
    steps, rows, width = tokens.shape
    hidden_width = up_weight.shape[1]
    blocks = active.shape[2]
    x = lax.axis_index("tensor") // NC
    slot = NZ * rows
    half = 2 * slot
    piece = half // NX
    up_bias = up_bias.astype(F32)
    down_bias = down_bias.astype(F32)

    opposite = shift(tokens.reshape(steps * rows, width), dy=2).reshape(tokens.shape)

    def start_rows(own):
        col = gather_z(own)
        return col, shift(col, dy=1), shift(col, dy=-1)

    def start_sums(col, prev, succ, far):
        own, away = up(col, prev, succ, far, up_weight)
        away = shift(away, dc=1)

        def piece_for(k):
            at = ((x + k) % NX) * piece
            return lax.dynamic_slice_in_dim(own, at, piece) + lax.dynamic_slice_in_dim(
                away, at, piece
            ).astype(F32)

        return piece_for(0), [piece_for(k).astype(BF16) for k in (1, -1, 2)]

    def activate(total, arrived, step):
        for part in arrived:
            total = total + part.astype(F32)
        mask = lax.dynamic_slice_in_dim(active[step], (x % 2) * 2, 2).astype(F32)
        preact = jnp.maximum(total + up_bias, 0.0)
        gated = preact.reshape(2, piece // 2, blocks, -1) * mask[:, None, :, None]
        return gated.reshape(piece, hidden_width).astype(BF16)

    def send_x(parts):
        return [shift(part, dx=k) for part, k in zip(parts, (1, -1, 2))]

    def combine_x(mine, arrived):
        near = jnp.zeros((half, hidden_width), BF16)
        near = lax.dynamic_update_slice_in_dim(near, mine, x * piece, 0)
        for part, k in zip(arrived, (1, -1, 2)):
            near = lax.dynamic_update_slice_in_dim(near, part, ((x - k) % NX) * piece, 0)
        return down(near, shift(near, dc=1), down_weight)

    def sum_z(part):
        return exchange_z(part.reshape(NZ, rows, width)).astype(F32).sum(0)

    col0, prev0, succ0 = start_rows(tokens[0])
    far0 = gather_z(opposite[0])
    total0, parts0 = start_sums(col0, prev0, succ0, far0)
    parts0, own1 = lax.optimization_barrier((parts0, tokens[1]))
    arrived0 = send_x(parts0)
    col1, prev1, succ1 = start_rows(own1)
    mine0 = activate(total0, arrived0, 0)
    mine0, opposite1 = lax.optimization_barrier((mine0, opposite[1]))
    hidden0 = send_x([mine0] * 3)
    far1 = gather_z(opposite1)
    outs0 = combine_x(mine0, hidden0)
    total1, parts1 = start_sums(col1, prev1, succ1, far1)
    parts1, outs0 = lax.optimization_barrier((parts1, outs0))
    arrived1 = send_x(parts1)
    back0 = [shift(outs0[1], dy=-1), shift(outs0[2], dy=1)]
    opposite0 = sum_z(outs0[3])
    mine1 = activate(total1, arrived1, 1)
    sent0 = (outs0[0] + back0[0].astype(F32) + back0[1].astype(F32)).astype(BF16)
    mine1, sent0, opposite0 = lax.optimization_barrier((mine1, sent0, opposite0))
    hidden1 = send_x([mine1] * 3)
    crossed0 = shift(opposite0.astype(BF16), dy=2)
    mixed0 = sum_z(sent0) + crossed0.astype(F32) + down_bias
    outs1 = combine_x(mine1, hidden1)
    back1 = [shift(outs1[1], dy=-1), shift(outs1[2], dy=1)]
    opposite1 = sum_z(outs1[3])
    sent1 = (outs1[0] + back1[0].astype(F32) + back1[1].astype(F32)).astype(BF16)
    sent1, opposite1 = lax.optimization_barrier((sent1, opposite1))
    crossed1 = shift(opposite1.astype(BF16), dy=2)
    mixed1 = sum_z(sent1) + crossed1.astype(F32) + down_bias
    return jnp.stack([mixed0.astype(BF16), mixed1.astype(BF16)])


def solution(mesh):
    placed = (
        P(None, "dp", "tensor"),
        P("tensor", "dp"),
        P("dp"),
        P("dp", "tensor"),
        P("tensor"),
        P(None, None, "dp"),
    )
    return jax.shard_map(
        local, mesh=mesh, in_specs=placed, out_specs=P(None, "dp", "tensor"), check_vma=False
    )
```

time: 722 us -> 221 us (0.31)
  waiting for transfers between devices: 672 us -> 98.4 us
  starting transfers between devices: 0.17 us -> 69.3 us
  matrix products: 28 us -> 0 us
  local copies, waits for them, and re-layouts: 2.74 us -> 21.7 us
  Pallas kernels: 0 us -> 18.6 us
  between operations: 13.2 us -> 0.45 us
    reduce_scatter x2 -> x0, waiting for transfers between devices: 436 us -> none  [local(): lax.psum_scatter(jnp.dot(hidden, down_weight, preferred_element_type=jnp....]
    all_gather x2 -> x0, waiting for transfers between devices: 151 us -> none  [local(): lax.all_gather(local_rows, 'dp', axis=0, tiled=True)]
    psum x1 -> x0, waiting for transfers between devices: 84 us -> none  [local(): summed = lax.psum(partial_up, 'tensor')]
    all_to_all x0 -> x8, waiting for transfers between devices: none -> 74.6 us  [exchange_z(): lax.all_to_all(blocks, 'dp', 0, 0, tiled=True, axis_index_groups=Z_GROUPS)]
    ppermute x0 -> x27, starting transfers between devices: none -> 35.2 us  [shift(): return lax.ppermute(value, AXES, pairs)]
    all_to_all x0 -> x8, starting transfers between devices: none -> 34.1 us  [exchange_z(): lax.all_to_all(blocks, 'dp', 0, 0, tiled=True, axis_index_groups=Z_GROUPS)]
    dot_general x6 -> x0, matrix products: 28 us -> none  [the longest x2 14.2 us: local(): jnp.dot(lax.all_gather(local_rows, 'dp', axis=0, tiled=True), up_weight,...]
    ppermute x0 -> x27, waiting for transfers between devices: none -> 23.8 us  [shift(): return lax.ppermute(value, AXES, pairs)]
  transfers between devices with their start and end apart: 5 -> 35, of which waited for: 5 -> 17; matrix products, arithmetic and copies ran while one was open for 2% -> 5% of each run, Pallas kernels for 0% -> 5%
where the time goes in v2:
time: 221 us; the launch traced here: 218 us
  waiting for transfers between devices  98.4 us (45%)
  starting transfers between devices  69.3 us (31%)
  local copies, waits for them, and re-layouts  21.7 us (10%)
  Pallas kernels  18.6 us (8%)
  other arithmetic  9.6 us (4%)
    all_to_all x8, waiting for transfers between devices, exchange_z(): lax.all_to_all(blocks, 'dp', 0, 0, tiled=True, axis_index_groups=Z_GROUPS)  74.6 us
    ppermute x27, starting transfers between devices, shift(): return lax.ppermute(value, AXES, pairs)  35.2 us
    all_to_all x8, starting transfers between devices, exchange_z(): lax.all_to_all(blocks, 'dp', 0, 0, tiled=True, axis_index_groups=Z_GROUPS)  34.1 us
    ppermute x27, waiting for transfers between devices, shift(): return lax.ppermute(value, AXES, pairs)  23.8 us
    unnamed x26, local copies, waits for them, and re-layouts  13.4 us
    pallas_call x2, Pallas kernels, down(): pl.pallas_call(down_kernel, grid=(width // TILE,), in_specs=[VMEM] * 2 +...  10.7 us
    pallas_call x2, Pallas kernels, up(): pl.pallas_call(up_kernel, grid=(width // TILE,), in_specs=[VMEM] * 4 + [p...  7.99 us
    broadcast_in_dim x4, local copies, waits for them, and re-layouts, gather_z(): copies = jnp.broadcast_to(block[None], (NZ,) + block.shape)  4.74 us
  transfers between devices with their start and end apart: 35, of which 17 were waited for; matrix products, arithmetic and copies ran while one was open for 5% of the time, Pallas kernels for 5%

profile of v2, /device:TPU:6, one launch (start us, length us, event | category | flops | bytes accessed | tf_op | source)
XLA Modules:
  0.0 218.1 jit_solution(7012821628470884505)
XLA Ops:
  2.2 8.5 %all-to-all-start = ((bf16[8,16,1536]{2,1,0:T(8,128)(2,1)}), bf16[8,16,1536]{2,1,0:T(8,128)(2,1)S(1)}, u32[]{:S(2)}, u32[]{:S(2)}) async-start(bf16[8,16,1536]{2,1,0:T(8,128)(2,1)} %broadcast_in_dim.11), calls=%async_computation | async-start | bytes 786432 | tf_op jit(solution)/shard_map/all_to_all | solution.py:30
  17.7 7.7 %all-to-all-done = bf16[8,16,1536]{2,1,0:T(8,128)(2,1)S(1)} async-done(((bf16[8,16,1536]{2,1,0:T(8,128)(2,1)}), bf16[8,16,1536]{2,1,0:T(8,128)(2,1)S(1)}, u32[]{:S(2)}, u32[]{:S(2)}) %all-to-all-start) | async-done | bytes 393248 | tf_op jit(solution)/shard_map/all_to_all | solution.py:30
  26.2 3.5 %all-to-all-start.1 = ((bf16[8,16,1536]{2,1,0:T(8,128)(2,1)}), bf16[8,16,1536]{2,1,0:T(8,128)(2,1)S(1)}, u32[]{:S(2)}, u32[]{:S(2)}) async-start(bf16[8,16,1536]{2,1,0:T(8,128)(2,1)} %broadcast_in_dim.12), calls=%async_computation.1 | async-start | bytes 786432 | tf_op jit(solution)/shard_map/all_to_all | solution.py:30
  32.9 10.8 %all-to-all-done.1 = bf16[8,16,1536]{2,1,0:T(8,128)(2,1)S(1)} async-done(((bf16[8,16,1536]{2,1,0:T(8,128)(2,1)}), bf16[8,16,1536]{2,1,0:T(8,128)(2,1)S(1)}, u32[]{:S(2)}, u32[]{:S(2)}) %all-to-all-start.1) | async-done | bytes 393248 | tf_op jit(solution)/shard_map/all_to_all | solution.py:30
  47.8 4.0 %shard_map.64 = (f32[256,1536]{1,0:T(8,128)S(1)}, bf16[256,1536]{1,0:T(8,128)(2,1)S(1)}) custom-call(bf16[128,1536]{1,0:T(8,128)(2,1)S(1)} %bitcast.39, bf16[128,1536]{1,0:T(8,128)(2,1)S(1)} %collective-permute-done.prev, bf16[128,1536]{1,0:T(8,128)(2,1)S(1)} %copy-done.7, bf16[128,1536]{1,0:T(8,128)(2,1)S(1)} %bitcast.40, bf16[1536,1536]{1,0:T(8,128)(2,1)S(1)} %copy-done), custom_call_target="tpu_custom_call" | custom-call | flops 2415919104 | bytes 4718592 | tf_op jit(solution)/shard_map/pallas_call | solution.py:63
  60.1 4.1 %all-to-all-start.2 = ((bf16[8,16,1536]{2,1,0:T(8,128)(2,1)}), bf16[8,16,1536]{2,1,0:T(8,128)(2,1)S(1)}, u32[]{:S(2)}, u32[]{:S(2)}) async-start(bf16[8,16,1536]{2,1,0:T(8,128)(2,1)} %broadcast_in_dim.13), calls=%async_computation.2 | async-start | bytes 786432 | tf_op jit(solution)/shard_map/all_to_all | solution.py:30
  64.2 3.4 %collective-permute-done.7 = bf16[64,1536]{1,0:T(8,128)(2,1)S(1)} collective-permute-done((bf16[64,1536]{1,0:T(8,128)(2,1)S(1)}, bf16[64,1536]{1,0:T(8,128)(2,1)S(1)}, u32[]{:S(2)}, u32[]{:S(2)}) %collective-permute-start.7) | collective-permute-done | bytes 196640 | tf_op jit(solution)/shard_map/ppermute | solution.py:26
  74.5 3.8 %all-to-all-done.2 = bf16[8,16,1536]{2,1,0:T(8,128)(2,1)S(1)} async-done(((bf16[8,16,1536]{2,1,0:T(8,128)(2,1)}), bf16[8,16,1536]{2,1,0:T(8,128)(2,1)S(1)}, u32[]{:S(2)}, u32[]{:S(2)}) %all-to-all-start.2) | async-done | bytes 393248 | tf_op jit(solution)/shard_map/all_to_all | solution.py:30
  79.9 3.5 %all-to-all-start.3 = ((bf16[8,16,1536]{2,1,0:T(8,128)(2,1)}), bf16[8,16,1536]{2,1,0:T(8,128)(2,1)S(1)}, u32[]{:S(2)}, u32[]{:S(2)}) async-start(bf16[8,16,1536]{2,1,0:T(8,128)(2,1)} %broadcast_in_dim.14), calls=%async_computation.3 | async-start | bytes 786432 | tf_op jit(solution)/shard_map/all_to_all | solution.py:30
  86.9 9.2 %all-to-all-done.3 = bf16[8,16,1536]{2,1,0:T(8,128)(2,1)S(1)} async-done(((bf16[8,16,1536]{2,1,0:T(8,128)(2,1)}), bf16[8,16,1536]{2,1,0:T(8,128)(2,1)S(1)}, u32[]{:S(2)}, u32[]{:S(2)}) %all-to-all-start.3) | async-done | bytes 393248 | tf_op jit(solution)/shard_map/all_to_all | solution.py:30
  100.2 4.0 %shard_map.65 = (f32[256,1536]{1,0:T(8,128)S(1)}, bf16[256,1536]{1,0:T(8,128)(2,1)S(1)}) custom-call(bf16[128,1536]{1,0:T(8,128)(2,1)S(1)} %bitcast.35, bf16[128,1536]{1,0:T(8,128)(2,1)S(1)} %collective-permute-done.4.prev, bf16[128,1536]{1,0:T(8,128)(2,1)S(1)} %copy-done.5, bf16[128,1536]{1,0:T(8,128)(2,1)S(1)} %bitcast.36, bf16[1536,1536]{1,0:T(8,128)(2,1)S(1)} %copy-done.1), custom_call_target="tpu_custom_call" | custom-call | flops 2415919104 | bytes 4718592 | tf_op jit(solution)/shard_map/pallas_call | solution.py:63
  106.8 5.9 %shard_map.66 = (f32[128,1536]{1,0:T(8,128)S(1)}, bf16[128,1536]{1,0:T(8,128)(2,1)}, bf16[128,1536]{1,0:T(8,128)(2,1)S(1)}, bf16[128,1536]{1,0:T(8,128)(2,1)}) custom-call(bf16[256,1536]{1,0:T(8,128)(2,1)S(1)} %constant_dynamic-update-slice_fusion.7.near, bf16[256,1536]{1,0:T(8,128)(2,1)} %collective-permute-done.13.other, bf16[1536,1536]{1,0:T(8,128)(2,1)S(1)} %copy-done.2), custom_call_target="tpu_custom_call" | custom-call | flops 2415919104 | bytes 4718592 | tf_op jit(solution)/shard_map/pallas_call | solution.py:103
  120.8 4.2 %all-to-all-start.4 = ((bf16[8,16,1536]{2,1,0:T(8,128)(2,1)}), bf16[8,16,1536]{2,1,0:T(8,128)(2,1)}, u32[]{:S(2)}, u32[]{:S(2)}) async-start(bf16[8,16,1536]{2,1,0:T(8,128)(2,1)} %bitcast.9), calls=%async_computation.4 | async-start | bytes 786432 | tf_op jit(solution)/shard_map/all_to_all | solution.py:30
  125.2 3.3 %collective-permute-done.15 = bf16[64,1536]{1,0:T(8,128)(2,1)S(1)} collective-permute-done((bf16[64,1536]{1,0:T(8,128)(2,1)}, bf16[64,1536]{1,0:T(8,128)(2,1)S(1)}, u32[]{:S(2)}, u32[]{:S(2)}) %collective-permute-start.15) | collective-permute-done | bytes 196640 | tf_op jit(solution)/shard_map/ppermute | solution.py:26
  134.4 5.0 %all-to-all-done.4 = bf16[8,16,1536]{2,1,0:T(8,128)(2,1)} async-done(((bf16[8,16,1536]{2,1,0:T(8,128)(2,1)}), bf16[8,16,1536]{2,1,0:T(8,128)(2,1)}, u32[]{:S(2)}, u32[]{:S(2)}) %all-to-all-start.4) | async-done | bytes 393248 | tf_op jit(solution)/shard_map/all_to_all | solution.py:30
  144.7 3.5 %collective-permute-done.20 = bf16[64,1536]{1,0:T(8,128)(2,1)S(1)} collective-permute-done((bf16[64,1536]{1,0:T(8,128)(2,1)S(1)}, bf16[64,1536]{1,0:T(8,128)(2,1)S(1)}, u32[]{:S(2)}, u32[]{:S(2)}) %collective-permute-start.20) | collective-permute-done | bytes 196640 | tf_op jit(solution)/shard_map/ppermute | solution.py:26
  148.2 3.9 %collective-permute-done.21 = bf16[64,1536]{1,0:T(8,128)(2,1)S(1)} collective-permute-done((bf16[64,1536]{1,0:T(8,128)(2,1)S(1)}, bf16[64,1536]{1,0:T(8,128)(2,1)S(1)}, u32[]{:S(2)}, u32[]{:S(2)}) %collective-permute-start.21) | collective-permute-done | bytes 196640 | tf_op jit(solution)/shard_map/ppermute | solution.py:26
  156.9 4.7 %shard_map.67 = (f32[128,1536]{1,0:T(8,128)S(1)}, bf16[128,1536]{1,0:T(8,128)(2,1)S(1)}, bf16[128,1536]{1,0:T(8,128)(2,1)S(1)}, bf16[128,1536]{1,0:T(8,128)(2,1)}) custom-call(bf16[256,1536]{1,0:T(8,128)(2,1)S(1)} %constant_dynamic-update-slice_fusion.3.near, bf16[256,1536]{1,0:T(8,128)(2,1)S(1)} %collective-permute-done.23.other, ...), custom_call_target="tpu_custom_call" | custom-call | flops 2415919104 | bytes 4718592 | tf_op jit(solution)/shard_map/pallas_call | solution.py:103
  161.6 3.5 %all-to-all-start.6 = ((bf16[8,16,1536]{2,1,0:T(8,128)(2,1)}), bf16[8,16,1536]{2,1,0:T(8,128)(2,1)S(1)}, u32[]{:S(2)}, u32[]{:S(2)}) async-start(bf16[8,16,1536]{2,1,0:T(8,128)(2,1)} %bitcast.12), calls=%async_computation.6 | async-start | bytes 786432 | tf_op jit(solution)/shard_map/all_to_all | solution.py:30
  167.6 12.7 %all-to-all-done.6 = bf16[8,16,1536]{2,1,0:T(8,128)(2,1)S(1)} async-done(((bf16[8,16,1536]{2,1,0:T(8,128)(2,1)}), bf16[8,16,1536]{2,1,0:T(8,128)(2,1)S(1)}, u32[]{:S(2)}, u32[]{:S(2)}) %all-to-all-start.6) | async-done | bytes 393248 | tf_op jit(solution)/shard_map/all_to_all | solution.py:30
  180.2 3.5 %all-to-all-start.5 = ((bf16[8,16,1536]{2,1,0:T(8,128)(2,1)}), bf16[8,16,1536]{2,1,0:T(8,128)(2,1)S(1)}, u32[]{:S(2)}, u32[]{:S(2)}) async-start(bf16[8,16,1536]{2,1,0:T(8,128)(2,1)} %bitcast.10), calls=%async_computation.5 | async-start | bytes 786432 | tf_op jit(solution)/shard_map/all_to_all | solution.py:30
  184.7 14.1 %all-to-all-done.5 = bf16[8,16,1536]{2,1,0:T(8,128)(2,1)S(1)} async-done(((bf16[8,16,1536]{2,1,0:T(8,128)(2,1)}), bf16[8,16,1536]{2,1,0:T(8,128)(2,1)S(1)}, u32[]{:S(2)}, u32[]{:S(2)}) %all-to-all-start.5) | async-done | bytes 393248 | tf_op jit(solution)/shard_map/all_to_all | solution.py:30
  198.8 3.5 %all-to-all-start.7 = ((bf16[8,16,1536]{2,1,0:T(8,128)(2,1)}), bf16[8,16,1536]{2,1,0:T(8,128)(2,1)S(1)}, u32[]{:S(2)}, u32[]{:S(2)}) async-start(bf16[8,16,1536]{2,1,0:T(8,128)(2,1)} %bitcast.13), calls=%async_computation.7 | async-start | bytes 786432 | tf_op jit(solution)/shard_map/all_to_all | solution.py:30
  206.0 11.3 %all-to-all-done.7 = bf16[8,16,1536]{2,1,0:T(8,128)(2,1)S(1)} async-done(((bf16[8,16,1536]{2,1,0:T(8,128)(2,1)}), bf16[8,16,1536]{2,1,0:T(8,128)(2,1)S(1)}, u32[]{:S(2)}, u32[]{:S(2)}) %all-to-all-start.7) | async-done | bytes 393248 | tf_op jit(solution)/shard_map/all_to_all | solution.py:30
  (110 shorter events, 76.3 us)
Async XLA Ops:
  2.2 23.2 %all-to-all-start = ((bf16[8,16,1536]{2,1,0:T(8,128)(2,1)}), bf16[8,16,1536]{2,1,0:T(8,128)(2,1)S(1)}, u32[]{:S(2)}, u32[]{:S(2)}) async-start(bf16[8,16,1536]{2,1,0:T(8,128)(2,1)} %broadcast_in_dim.11), calls=%async_computation | async-start | bytes 786432 | tf_op jit(solution)/shard_map/all_to_all | solution.py:30
  26.2 17.6 %all-to-all-start.1 = ((bf16[8,16,1536]{2,1,0:T(8,128)(2,1)}), bf16[8,16,1536]{2,1,0:T(8,128)(2,1)S(1)}, u32[]{:S(2)}, u32[]{:S(2)}) async-start(bf16[8,16,1536]{2,1,0:T(8,128)(2,1)} %broadcast_in_dim.12), calls=%async_computation.1 | async-start | bytes 786432 | tf_op jit(solution)/shard_map/all_to_all | solution.py:30
  29.6 14.1 %collective-permute-start = (bf16[128,1536]{1,0:T(8,128)(2,1)S(1)}, bf16[128,1536]{1,0:T(8,128)(2,1)S(1)}, u32[]{:S(2)}, u32[]{:S(2)}) collective-permute-start(bf16[128,1536]{1,0:T(8,128)(2,1)S(1)} %bitcast.37), channel_id=1, source_target_pairs={{0,8},{1,9},{2,10},{3,11},{4,12},{5,13},{6,14},{7,15},{8,16},{9,17... | collective-permute-start | bytes 1179656 | tf_op jit(solution)/shard_map/ppermute | solution.py:26
  31.3 12.5 %collective-permute-start.1 = (bf16[128,1536]{1,0:T(8,128)(2,1)S(1)}, bf16[128,1536]{1,0:T(8,128)(2,1)S(1)}, u32[]{:S(2)}, u32[]{:S(2)}) collective-permute-start(bf16[128,1536]{1,0:T(8,128)(2,1)S(1)} %bitcast.38), channel_id=1, source_target_pairs={{0,24},{1,25},{2,26},{3,27},{4,28},{5,29},{6,30},{7,31},{8,0},{9,1... | collective-permute-start | bytes 1179656 | tf_op jit(solution)/shard_map/ppermute | solution.py:26
  55.5 12.1 %collective-permute-start.7 = (bf16[64,1536]{1,0:T(8,128)(2,1)S(1)}, bf16[64,1536]{1,0:T(8,128)(2,1)S(1)}, u32[]{:S(2)}, u32[]{:S(2)}) collective-permute-start(bf16[64,1536]{1,0:T(8,128)(2,1)S(1)} %get-tuple-element.39), channel_id=1, source_target_pairs={{0,6},{1,7},{2,0},{3,1},{4,2},{5,3},{6,4},{7,5},{8,14},{9,15},{10,... | collective-permute-start | bytes 589832 | tf_op jit(solution)/shard_map/ppermute | solution.py:26
  60.1 18.3 %all-to-all-start.2 = ((bf16[8,16,1536]{2,1,0:T(8,128)(2,1)}), bf16[8,16,1536]{2,1,0:T(8,128)(2,1)S(1)}, u32[]{:S(2)}, u32[]{:S(2)}) async-start(bf16[8,16,1536]{2,1,0:T(8,128)(2,1)} %broadcast_in_dim.13), calls=%async_computation.2 | async-start | bytes 786432 | tf_op jit(solution)/shard_map/all_to_all | solution.py:30
  69.6 13.9 %collective-permute-start.10 = (bf16[64,1536]{1,0:T(8,128)(2,1)}, bf16[64,1536]{1,0:T(8,128)(2,1)S(1)}, u32[]{:S(2)}, u32[]{:S(2)}) collective-permute-start(bf16[64,1536]{1,0:T(8,128)(2,1)} %fusion.1), channel_id=1, source_target_pairs={{0,2},{1,3},{2,4},{3,5},{4,6},{5,7},{6,0},{7,1},{8,10},{9,11},{10,... | collective-permute-start | bytes 589832 | tf_op jit(solution)/shard_map/ppermute | solution.py:26
  71.1 15.6 %collective-permute-start.11 = (bf16[64,1536]{1,0:T(8,128)(2,1)}, bf16[64,1536]{1,0:T(8,128)(2,1)S(1)}, u32[]{:S(2)}, u32[]{:S(2)}) collective-permute-start(bf16[64,1536]{1,0:T(8,128)(2,1)} %fusion.1), channel_id=1, source_target_pairs={{0,6},{1,7},{2,0},{3,1},{4,2},{5,3},{6,4},{7,5},{8,14},{9,15},{10,... | collective-permute-start | bytes 589832 | tf_op jit(solution)/shard_map/ppermute | solution.py:26
  71.6 15.2 %collective-permute-start.12 = (bf16[64,1536]{1,0:T(8,128)(2,1)}, bf16[64,1536]{1,0:T(8,128)(2,1)S(1)}, u32[]{:S(2)}, u32[]{:S(2)}) collective-permute-start(bf16[64,1536]{1,0:T(8,128)(2,1)} %fusion.1), channel_id=1, source_target_pairs={{0,4},{1,5},{2,6},{3,7},{4,0},{5,1},{6,2},{7,3},{8,12},{9,13},{10,... | collective-permute-start | bytes 589832 | tf_op jit(solution)/shard_map/ppermute | solution.py:26
  79.9 16.2 %all-to-all-start.3 = ((bf16[8,16,1536]{2,1,0:T(8,128)(2,1)}), bf16[8,16,1536]{2,1,0:T(8,128)(2,1)S(1)}, u32[]{:S(2)}, u32[]{:S(2)}) async-start(bf16[8,16,1536]{2,1,0:T(8,128)(2,1)} %broadcast_in_dim.14), calls=%async_computation.3 | async-start | bytes 786432 | tf_op jit(solution)/shard_map/all_to_all | solution.py:30
  83.4 12.7 %collective-permute-start.4 = (bf16[128,1536]{1,0:T(8,128)(2,1)S(1)}, bf16[128,1536]{1,0:T(8,128)(2,1)S(1)}, u32[]{:S(2)}, u32[]{:S(2)}) collective-permute-start(bf16[128,1536]{1,0:T(8,128)(2,1)S(1)} %bitcast.33), channel_id=1, source_target_pairs={{0,8},{1,9},{2,10},{3,11},{4,12},{5,13},{6,14},{7,15},{8,16},{9,17... | collective-permute-start | bytes 1179656 | tf_op jit(solution)/shard_map/ppermute | solution.py:26
  86.8 17.7 %collective-permute-start.13 = (bf16[256,1536]{1,0:T(8,128)(2,1)S(1)}, bf16[256,1536]{1,0:T(8,128)(2,1)}, u32[]{:S(2)}, u32[]{:S(2)}) collective-permute-start(bf16[256,1536]{1,0:T(8,128)(2,1)S(1)} %constant_dynamic-update-slice_fusion.7.near), channel_id=1, source_target_pairs={{0,1},{1,0},{2,3},{3,2},{4,5},{5,4},{6,7},{7,6},{8,9},{9,8},{10,11... | collective-permute-start | bytes 2359304 | tf_op jit(solution)/shard_map/ppermute | solution.py:26
  115.8 12.6 %collective-permute-start.15 = (bf16[64,1536]{1,0:T(8,128)(2,1)}, bf16[64,1536]{1,0:T(8,128)(2,1)S(1)}, u32[]{:S(2)}, u32[]{:S(2)}) collective-permute-start(bf16[64,1536]{1,0:T(8,128)(2,1)} %get-tuple-element.50), channel_id=1, source_target_pairs={{0,6},{1,7},{2,0},{3,1},{4,2},{5,3},{6,4},{7,5},{8,14},{9,15},{10,... | collective-permute-start | bytes 589832 | tf_op jit(solution)/shard_map/ppermute | solution.py:26
  115.8 12.7 %collective-permute-start.16 = (bf16[64,1536]{1,0:T(8,128)(2,1)}, bf16[64,1536]{1,0:T(8,128)(2,1)}, u32[]{:S(2)}, u32[]{:S(2)}) collective-permute-start(bf16[64,1536]{1,0:T(8,128)(2,1)} %get-tuple-element.51), channel_id=1, source_target_pairs={{0,4},{1,5},{2,6},{3,7},{4,0},{5,1},{6,2},{7,3},{8,12},{9,13},{10,... | collective-permute-start | bytes 589832 | tf_op jit(solution)/shard_map/ppermute | solution.py:26
  117.9 12.6 %collective-permute-start.17 = (bf16[128,1536]{1,0:T(8,128)(2,1)}, bf16[128,1536]{1,0:T(8,128)(2,1)S(1)}, u32[]{:S(2)}, u32[]{:S(2)}) collective-permute-start(bf16[128,1536]{1,0:T(8,128)(2,1)} %get-tuple-element.53), channel_id=1, source_target_pairs={{0,24},{1,25},{2,26},{3,27},{4,28},{5,29},{6,30},{7,31},{8,0},{9,1... | collective-permute-start | bytes 1179656 | tf_op jit(solution)/shard_map/ppermute | solution.py:26
  120.8 11.7 %collective-permute-start.18 = (bf16[128,1536]{1,0:T(8,128)(2,1)S(1)}, bf16[128,1536]{1,0:T(8,128)(2,1)}, u32[]{:S(2)}, u32[]{:S(2)}) collective-permute-start(bf16[128,1536]{1,0:T(8,128)(2,1)S(1)} %get-tuple-element.54), channel_id=1, source_target_pairs={{0,8},{1,9},{2,10},{3,11},{4,12},{5,13},{6,14},{7,15},{8,16},{9,17... | collective-permute-start | bytes 1179656 | tf_op jit(solution)/shard_map/ppermute | solution.py:26
  120.8 18.6 %all-to-all-start.4 = ((bf16[8,16,1536]{2,1,0:T(8,128)(2,1)}), bf16[8,16,1536]{2,1,0:T(8,128)(2,1)}, u32[]{:S(2)}, u32[]{:S(2)}) async-start(bf16[8,16,1536]{2,1,0:T(8,128)(2,1)} %bitcast.9), calls=%async_computation.4 | async-start | bytes 786432 | tf_op jit(solution)/shard_map/all_to_all | solution.py:30
  161.6 18.6 %all-to-all-start.6 = ((bf16[8,16,1536]{2,1,0:T(8,128)(2,1)}), bf16[8,16,1536]{2,1,0:T(8,128)(2,1)S(1)}, u32[]{:S(2)}, u32[]{:S(2)}) async-start(bf16[8,16,1536]{2,1,0:T(8,128)(2,1)} %bitcast.12), calls=%async_computation.6 | async-start | bytes 786432 | tf_op jit(solution)/shard_map/all_to_all | solution.py:30
  165.1 18.6 %collective-permute-start.24 = (bf16[128,1536]{1,0:T(8,128)(2,1)S(1)}, bf16[128,1536]{1,0:T(8,128)(2,1)S(1)}, u32[]{:S(2)}, u32[]{:S(2)}) collective-permute-start(bf16[128,1536]{1,0:T(8,128)(2,1)S(1)} %get-tuple-element.60), channel_id=1, source_target_pairs={{0,24},{1,25},{2,26},{3,27},{4,28},{5,29},{6,30},{7,31},{8,0},{9,1... | collective-permute-start | bytes 1179656 | tf_op jit(solution)/shard_map/ppermute | solution.py:26
  167.6 16.2 %collective-permute-start.25 = (bf16[128,1536]{1,0:T(8,128)(2,1)S(1)}, bf16[128,1536]{1,0:T(8,128)(2,1)S(1)}, u32[]{:S(2)}, u32[]{:S(2)}) collective-permute-start(bf16[128,1536]{1,0:T(8,128)(2,1)S(1)} %get-tuple-element.61), channel_id=1, source_target_pairs={{0,8},{1,9},{2,10},{3,11},{4,12},{5,13},{6,14},{7,15},{8,16},{9,17... | collective-permute-start | bytes 1179656 | tf_op jit(solution)/shard_map/ppermute | solution.py:26
  180.2 18.5 %all-to-all-start.5 = ((bf16[8,16,1536]{2,1,0:T(8,128)(2,1)}), bf16[8,16,1536]{2,1,0:T(8,128)(2,1)S(1)}, u32[]{:S(2)}, u32[]{:S(2)}) async-start(bf16[8,16,1536]{2,1,0:T(8,128)(2,1)} %bitcast.10), calls=%async_computation.5 | async-start | bytes 786432 | tf_op jit(solution)/shard_map/all_to_all | solution.py:30
  198.8 18.5 %all-to-all-start.7 = ((bf16[8,16,1536]{2,1,0:T(8,128)(2,1)}), bf16[8,16,1536]{2,1,0:T(8,128)(2,1)S(1)}, u32[]{:S(2)}, u32[]{:S(2)}) async-start(bf16[8,16,1536]{2,1,0:T(8,128)(2,1)} %bitcast.13), calls=%async_computation.7 | async-start | bytes 786432 | tf_op jit(solution)/shard_map/all_to_all | solution.py:30
  202.3 15.1 %collective-permute-start.19 = (bf16[16,1536]{1,0:T(8,128)(2,1)S(1)}, bf16[16,1536]{1,0:T(8,128)(2,1)S(1)}, u32[]{:S(2)}, u32[]{:S(2)}) collective-permute-start(bf16[16,1536]{1,0:T(8,128)(2,1)S(1)} %convert_reduce_fusion.3), channel_id=1, source_target_pairs={{0,16},{1,17},{2,18},{3,19},{4,20},{5,21},{6,22},{7,23},{8,24},{9,... | collective-permute-start | bytes 147464 | tf_op jit(solution)/shard_map/ppermute | solution.py:26
  203.7 13.7 %collective-permute-start.26 = (bf16[16,1536]{1,0:T(8,128)(2,1)S(1)}, bf16[16,1536]{1,0:T(8,128)(2,1)S(1)}, u32[]{:S(2)}, u32[]{:S(2)}) collective-permute-start(bf16[16,1536]{1,0:T(8,128)(2,1)S(1)} %convert_reduce_fusion.1), channel_id=1, source_target_pairs={{0,16},{1,17},{2,18},{3,19},{4,20},{5,21},{6,22},{7,23},{8,24},{9,... | collective-permute-start | bytes 147464 | tf_op jit(solution)/shard_map/ppermute | solution.py:26
  (24 other events, 142.3 us)

commit v3 on v0

v3 whole, which is shorter than its diff:
```python
import jax
import jax.numpy as jnp
from jax import lax
from jax.experimental import pallas as pl
from jax.experimental.pallas import tpu as pltpu
from jax.sharding import PartitionSpec as P

AXES = ("dp", "tensor")
NZ, NY, NX, NC = 8, 4, 4, 2
Z_GROUPS = [[z * NY + y for z in range(NZ)] for y in range(NY)]
F32 = jnp.float32
BF16 = jnp.bfloat16
TILE = 256


def shift(value, dz=0, dy=0, dx=0, dc=0):
    pairs = []
    for z in range(NZ):
        for y in range(NY):
            for x in range(NX):
                for c in range(NC):
                    source = ((z * NY + y) * NX + x) * NC + c
                    zt, yt, xt, ct = (z + dz) % NZ, (y + dy) % NY, (x + dx) % NX, (c + dc) % NC
                    pairs.append((source, ((zt * NY + yt) * NX + xt) * NC + ct))
    return lax.ppermute(value, AXES, pairs)


def exchange_z(blocks):
    return lax.all_to_all(blocks, "dp", 0, 0, tiled=True, axis_index_groups=Z_GROUPS)


def gather_z(block):
    copies = jnp.broadcast_to(block[None], (NZ,) + block.shape)
    return exchange_z(copies).reshape(NZ * block.shape[0], block.shape[1])


def up_kernel(col, prev, succ, far, weight, own, away):
    rows = own.shape[1] // NZ
    for i, slot in enumerate((col, prev, succ, far)):
        product = jnp.dot(slot[...], weight[...], preferred_element_type=F32)
        for z in range(NZ):
            at = 2 * z * rows
            own[i, z * rows : (z + 1) * rows] = product[at : at + rows]
            away[i, z * rows : (z + 1) * rows] = product[at + rows : at + 2 * rows].astype(BF16)


def up(slots, weight):
    size, depth = slots[0].shape
    width = weight.shape[1]
    shape = (NY, size // 2, width)
    return pl.pallas_call(
        up_kernel,
        grid=(width // TILE,),
        in_specs=[pl.BlockSpec((size, depth), lambda j: (0, 0))] * 4
        + [pl.BlockSpec((depth, TILE), lambda j: (0, j))],
        out_specs=[pl.BlockSpec((NY, size // 2, TILE), lambda j: (0, 0, j))] * 2,
        out_shape=[jax.ShapeDtypeStruct(shape, F32), jax.ShapeDtypeStruct(shape, BF16)],
        compiler_params=pltpu.CompilerParams(vmem_limit_bytes=58 * 2**20),
        cost_estimate=pl.CostEstimate(
            flops=8 * size * depth * width, bytes_accessed=2 * depth * width, transcendentals=0
        ),
    )(*slots, weight)


def down_kernel(near, other, weight, *outs):
    size = near.shape[1]
    rows = size // NZ
    for t, source in enumerate((near, other)):
        hidden = source[...].reshape(NY * size, source.shape[2])
        product = jnp.dot(hidden, weight[...], preferred_element_type=F32)
        for i, out in enumerate(outs):
            for z in range(NZ):
                at = i * size + z * rows
                to = (2 * z + t) * rows
                out[to : to + rows] = product[at : at + rows].astype(out.dtype)


def down(near, other, weight):
    _, size, depth = near.shape
    width = weight.shape[1]
    return pl.pallas_call(
        down_kernel,
        grid=(width // TILE,),
        in_specs=[pl.BlockSpec((NY, size, depth), lambda j: (0, 0, 0))] * 2
        + [pl.BlockSpec((depth, TILE), lambda j: (0, j))],
        out_specs=[pl.BlockSpec((2 * size, TILE), lambda j: (0, j))] * 4,
        out_shape=[jax.ShapeDtypeStruct((2 * size, width), F32)]
        + [jax.ShapeDtypeStruct((2 * size, width), BF16)] * 3,
        compiler_params=pltpu.CompilerParams(vmem_limit_bytes=58 * 2**20),
        cost_estimate=pl.CostEstimate(
            flops=16 * size * depth * width, bytes_accessed=2 * depth * width, transcendentals=0
        ),
    )(near, other, weight)


def local(tokens, up_weight, up_bias, down_weight, down_bias, active):
    steps, rows, width = tokens.shape
    hidden_width = up_weight.shape[1]
    blocks = active.shape[2]
    x = lax.axis_index("tensor") // NC
    c = lax.axis_index("tensor") % NC
    up_bias = up_bias.astype(F32)
    down_bias = down_bias.astype(F32)

    own = jnp.where(c == 0, tokens, tokens[::-1]).reshape(steps * rows, width)
    opposite = shift(own, dy=2)
    col = gather_z(own)
    prev, succ = shift(col, dy=1), shift(col, dy=-1)
    far = gather_z(opposite)

    mine, away = up((col, prev, succ, far), up_weight)
    away = shift(away, dc=1)

    def slot_for(k):
        at = (x + k) % NX
        return mine[at] + away[at].astype(F32)

    sends = (1, -1, 2)
    total = slot_for(0)
    for k in sends:
        total = total + shift(slot_for(k).astype(BF16), dx=k).astype(F32)
    mask = jnp.repeat(active[c].astype(F32), 2, axis=0)
    preact = jnp.maximum(total + up_bias, 0.0)
    gated = preact.reshape(NZ, rows, blocks, -1) * mask[:, None, :, None]
    gated = gated.reshape(NZ * rows, hidden_width).astype(BF16)

    near = jnp.zeros((NX,) + gated.shape, BF16)
    near = lax.dynamic_update_index_in_dim(near, gated, x, 0)
    for k in sends:
        near = lax.dynamic_update_index_in_dim(near, shift(gated, dx=k), (x - k) % NX, 0)
    outs = down(near, shift(near, dc=1), down_weight)

    def sum_z(part):
        return exchange_z(part.reshape(NZ, steps * rows, width)).astype(F32).sum(0)

    back = [shift(outs[1], dy=-1), shift(outs[2], dy=1)]
    crossed = shift(sum_z(outs[3]).astype(BF16), dy=2)
    summed = outs[0] + back[0].astype(F32) + back[1].astype(F32)
    mixed = (sum_z(summed.astype(BF16)) + crossed.astype(F32) + down_bias).astype(BF16)
    mixed = mixed.reshape(tokens.shape)
    return jnp.where(c == 0, mixed, mixed[::-1])


def solution(mesh):
    placed = (
        P(None, "dp", "tensor"),
        P("tensor", "dp"),
        P("dp"),
        P("dp", "tensor"),
        P("tensor"),
        P(None, None, "dp"),
    )
    return jax.shard_map(
        local, mesh=mesh, in_specs=placed, out_specs=P(None, "dp", "tensor"), check_vma=False
    )
```

time: 722 us -> 200 us (0.28)
  waiting for transfers between devices: 672 us -> 125 us
  starting transfers between devices: 0.17 us -> 39.6 us
  matrix products: 28 us -> 0 us
  Pallas kernels: 0 us -> 19.6 us
  between operations: 13.2 us -> 0.18 us
    reduce_scatter x2 -> x0, waiting for transfers between devices: 436 us -> none  [local(): lax.psum_scatter(jnp.dot(hidden, down_weight, preferred_element_type=jnp....]
    all_gather x2 -> x0, waiting for transfers between devices: 151 us -> none  [local(): lax.all_gather(local_rows, 'dp', axis=0, tiled=True)]
    psum x1 -> x0, waiting for transfers between devices: 84 us -> none  [local(): summed = lax.psum(partial_up, 'tensor')]
    ppermute x0 -> x14, waiting for transfers between devices: none -> 65.7 us  [shift(): return lax.ppermute(value, AXES, pairs)]
    all_to_all x0 -> x4, waiting for transfers between devices: none -> 58.9 us  [exchange_z(): lax.all_to_all(blocks, 'dp', 0, 0, tiled=True, axis_index_groups=Z_GROUPS)]
    dot_general x6 -> x0, matrix products: 28 us -> none  [the longest x2 14.2 us: local(): jnp.dot(lax.all_gather(local_rows, 'dp', axis=0, tiled=True), up_weight,...]
    all_to_all x0 -> x4, starting transfers between devices: none -> 22.8 us  [exchange_z(): lax.all_to_all(blocks, 'dp', 0, 0, tiled=True, axis_index_groups=Z_GROUPS)]
    pallas_call x0 -> x2, Pallas kernels: none -> 19.6 us  [the longest x1 10 us: up(): pl.pallas_call(up_kernel, grid=(width // TILE,), in_specs=[pl.BlockSpec((...]
  transfers between devices with their start and end apart: 5 -> 18, of which waited for: 5 -> 12; matrix products, arithmetic and copies ran while one was open for 2% -> 1% of each run, Pallas kernels for 0% -> 0%
where the time goes in v3:
time: 200 us; the launch traced here: 199 us
  waiting for transfers between devices  125 us (62%)
  starting transfers between devices  39.6 us (20%)
  Pallas kernels  19.6 us (10%)
  other arithmetic  8.33 us (4%)
  local copies, waits for them, and re-layouts  6.63 us (3%)
    ppermute x14, waiting for transfers between devices, shift(): return lax.ppermute(value, AXES, pairs)  65.7 us
    all_to_all x4, waiting for transfers between devices, exchange_z(): lax.all_to_all(blocks, 'dp', 0, 0, tiled=True, axis_index_groups=Z_GROUPS)  58.9 us
    all_to_all x4, starting transfers between devices, exchange_z(): lax.all_to_all(blocks, 'dp', 0, 0, tiled=True, axis_index_groups=Z_GROUPS)  22.8 us
    ppermute x14, starting transfers between devices, shift(): return lax.ppermute(value, AXES, pairs)  16.7 us
    pallas_call x1, Pallas kernels, up(): pl.pallas_call(up_kernel, grid=(width // TILE,), in_specs=[pl.BlockSpec((...  10 us
    pallas_call x1, Pallas kernels, down(): pl.pallas_call(down_kernel, grid=(width // TILE,), in_specs=[pl.BlockSpec...  9.64 us
    unnamed x28, local copies, waits for them, and re-layouts  4.28 us
  transfers between devices with their start and end apart: 18, of which 12 were waited for; matrix products, arithmetic and copies ran while one was open for 1% of the time, Pallas kernels for 0%

profile of v3, /device:TPU:6, one launch (start us, length us, event | category | flops | bytes accessed | tf_op | source)
XLA Modules:
  0.0 198.9 jit_solution(14994189934229425664)
XLA Ops:
  2.0 8.5 %all-to-all-start = ((bf16[8,32,1536]{2,1,0:T(8,128)(2,1)}), bf16[8,32,1536]{2,1,0:T(8,128)(2,1)S(1)}, u32[]{:S(2)}, u32[]{:S(2)}) async-start(bf16[8,32,1536]{2,1,0:T(8,128)(2,1)} %broadcast_in_dim.36), calls=%async_computation | async-start | bytes 1572864 | tf_op jit(solution)/shard_map/all_to_all | solution.py:29
  10.4 3.2 %collective-permute-start.2 = (bf16[32,1536]{1,0:T(8,128)(2,1)S(1)}, bf16[32,1536]{1,0:T(8,128)(2,1)S(1)}, u32[]{:S(2)}, u32[]{:S(2)}) collective-permute-start(bf16[32,1536]{1,0:T(8,128)(2,1)S(1)} %bitcast.50), channel_id=1, source_target_pairs={{0,16},{1,17},{2,18},{3,19},{4,20},{5,21},{6,22},{7,23},{8,24},{9,... | collective-permute-start | bytes 294920 | tf_op jit(solution)/shard_map/ppermute | solution.py:25
  13.6 2.9 %collective-permute-done.2 = bf16[32,1536]{1,0:T(8,128)(2,1)S(1)} collective-permute-done((bf16[32,1536]{1,0:T(8,128)(2,1)S(1)}, bf16[32,1536]{1,0:T(8,128)(2,1)S(1)}, u32[]{:S(2)}, u32[]{:S(2)}) %collective-permute-start.2) | collective-permute-done | bytes 98336 | tf_op jit(solution)/shard_map/ppermute | solution.py:25
  16.6 17.0 %all-to-all-done = bf16[8,32,1536]{2,1,0:T(8,128)(2,1)S(1)} async-done(((bf16[8,32,1536]{2,1,0:T(8,128)(2,1)}), bf16[8,32,1536]{2,1,0:T(8,128)(2,1)S(1)}, u32[]{:S(2)}, u32[]{:S(2)}) %all-to-all-start) | async-done | bytes 786464 | tf_op jit(solution)/shard_map/all_to_all | solution.py:29
  34.6 3.5 %all-to-all-start.1 = ((bf16[8,32,1536]{2,1,0:T(8,128)(2,1)}), bf16[8,32,1536]{2,1,0:T(8,128)(2,1)S(1)}, u32[]{:S(2)}, u32[]{:S(2)}) async-start(bf16[8,32,1536]{2,1,0:T(8,128)(2,1)} %broadcast_in_dim.37), calls=%async_computation.1 | async-start | bytes 1572864 | tf_op jit(solution)/shard_map/all_to_all | solution.py:29
  39.8 1.7 collective-permute-start.1
  41.5 20.2 %all-to-all-done.1 = bf16[8,32,1536]{2,1,0:T(8,128)(2,1)S(1)} async-done(((bf16[8,32,1536]{2,1,0:T(8,128)(2,1)}), bf16[8,32,1536]{2,1,0:T(8,128)(2,1)S(1)}, u32[]{:S(2)}, u32[]{:S(2)}) %all-to-all-start.1) | async-done | bytes 786464 | tf_op jit(solution)/shard_map/all_to_all | solution.py:29
  63.1 10.0 %shard_map.64 = (f32[4,128,1536]{2,1,0:T(8,128)}, bf16[4,128,1536]{2,1,0:T(8,128)(2,1)}) custom-call(bf16[256,1536]{1,0:T(8,128)(2,1)} %bitcast.46, bf16[256,1536]{1,0:T(8,128)(2,1)} %copy-done.12, bf16[256,1536]{1,0:T(8,128)(2,1)} %copy-done.13, bf16[256,1536]{1,0:T(8,128)(2,1)} %bitcast.48, bf16[1536,1536]{1,0:T(8,128)(2,1)} %weight.2), custom_call_target="tpu_custom_call" | custom-call | flops 4831838208 | bytes 4718592 | tf_op jit(solution)/shard_map/pallas_call | solution.py:51
  73.1 3.6 %collective-permute-done.3 = bf16[4,128,1536]{2,1,0:T(8,128)(2,1)S(1)} collective-permute-done((bf16[4,128,1536]{2,1,0:T(8,128)(2,1)}, bf16[4,128,1536]{2,1,0:T(8,128)(2,1)S(1)}, u32[]{:S(2)}, u32[]{:S(2)}) %collective-permute-start.3) | collective-permute-done | bytes 1572896 | tf_op jit(solution)/shard_map/ppermute | solution.py:25
  76.7 2.7 %fusion.5 = (bf16[128,1536]{1,0:T(8,128)(2,1)}, bf16[128,1536]{1,0:T(8,128)(2,1)S(1)}, bf16[128,1536]{1,0:T(8,128)(2,1)S(1)}) fusion(f32[4,128,1536]{2,1,0:T(8,128)} %get-tuple-element.11, s32[]{:T(128)S(6)} %select_n.82, bf16[4,128,1536]{2,1,0:T(8,128)(2,1)S(1)} %collective-permute-done.3, s32[]{:T(128)S(6)} %select_n.86, s32[]{:T(128)S(6)} %select_n.84), kind=kLoop, calls=%fused_computation.12 | loop fusion | flops 1769472 | bytes 4718604 | tf_op jit(solution)/shard_map/convert_element_type | solution.py:121
  82.9 8.7 %collective-permute-done.4 = bf16[128,1536]{1,0:T(8,128)(2,1)S(1)} collective-permute-done((bf16[128,1536]{1,0:T(8,128)(2,1)}, bf16[128,1536]{1,0:T(8,128)(2,1)S(1)}, u32[]{:S(2)}, u32[]{:S(2)}) %collective-permute-start.4) | collective-permute-done | bytes 393248 | tf_op jit(solution)/shard_map/ppermute | solution.py:25
  91.6 8.8 %collective-permute-done.5 = bf16[128,1536]{1,0:T(8,128)(2,1)S(1)} collective-permute-done((bf16[128,1536]{1,0:T(8,128)(2,1)S(1)}, bf16[128,1536]{1,0:T(8,128)(2,1)S(1)}, u32[]{:S(2)}, u32[]{:S(2)}) %collective-permute-start.5) | collective-permute-done | bytes 393248 | tf_op jit(solution)/shard_map/ppermute | solution.py:25
  102.4 2.5 %bitcast_dynamic-update-slice_fusion.3 = (bf16[4,128,1536]{2,1,0:T(8,128)(2,1)S(1)}, bf16[128,1536]{1,0:T(8,128)(2,1)}) fusion(bf16[4,128,1536]{2,1,0:T(8,128)(2,1)S(1)} %broadcast_in_dim.34, s32[]{:T(128)S(6)} %select_n.88, f32[16,8,12,128]{3,2,1,0:T(8,128)S(1)} %bitcast.43, f32[1536]{0:T(1024)S(1)} %convert_element_type.91, ...), kind=kLoop, calls=%fused_computation.18 | loop fusion | flops 2359296 | bytes 4202504 | tf_op jit(solution)/shard_map/jit(dynamic_update_index_in_dim)/dynamic_update_slice | solution.py:128
  106.9 1.7 collective-permute-start.9
  108.6 14.2 %collective-permute-done.7 = bf16[128,1536]{1,0:T(8,128)(2,1)S(1)} collective-permute-done((bf16[128,1536]{1,0:T(8,128)(2,1)}, bf16[128,1536]{1,0:T(8,128)(2,1)S(1)}, u32[]{:S(2)}, u32[]{:S(2)}) %collective-permute-start.7) | collective-permute-done | bytes 393248 | tf_op jit(solution)/shard_map/ppermute | solution.py:25
  122.9 3.2 %collective-permute-done.8 = bf16[128,1536]{1,0:T(8,128)(2,1)S(1)} collective-permute-done((bf16[128,1536]{1,0:T(8,128)(2,1)}, bf16[128,1536]{1,0:T(8,128)(2,1)S(1)}, u32[]{:S(2)}, u32[]{:S(2)}) %collective-permute-start.8) | collective-permute-done | bytes 393248 | tf_op jit(solution)/shard_map/ppermute | solution.py:25
  126.3 3.4 %collective-permute-done.10.other = bf16[4,128,1536]{2,1,0:T(8,128)(2,1)S(1)} collective-permute-done((bf16[4,128,1536]{2,1,0:T(8,128)(2,1)S(1)}, bf16[4,128,1536]{2,1,0:T(8,128)(2,1)S(1)}, u32[]{:S(2)}, u32[]{:S(2)}) %collective-permute-start.10) | collective-permute-done | bytes 1572896 | tf_op jit(solution)/shard_map/ppermute | solution.py:25
  130.9 9.6 %shard_map.65 = (f32[256,1536]{1,0:T(8,128)}, bf16[256,1536]{1,0:T(8,128)(2,1)}, bf16[256,1536]{1,0:T(8,128)(2,1)}, bf16[256,1536]{1,0:T(8,128)(2,1)}) custom-call(bf16[4,128,1536]{2,1,0:T(8,128)(2,1)} %copy-done, bf16[4,128,1536]{2,1,0:T(8,128)(2,1)} %copy-done.11, bf16[1536,1536]{1,0:T(8,128)(2,1)} %weight.3), custom_call_target="tpu_custom_call" | custom-call | flops 4831838208 | bytes 4718592 | tf_op jit(solution)/shard_map/pallas_call | solution.py:81
  140.5 3.9 %all-to-all-start.3 = ((bf16[8,32,1536]{2,1,0:T(8,128)(2,1)}), bf16[8,32,1536]{2,1,0:T(8,128)(2,1)S(1)}, u32[]{:S(2)}, u32[]{:S(2)}) async-start(bf16[8,32,1536]{2,1,0:T(8,128)(2,1)} %bitcast.47), calls=%async_computation.3 | async-start | bytes 1572864 | tf_op jit(solution)/shard_map/all_to_all | solution.py:29
  144.5 2.8 %collective-permute-start.11 = (bf16[256,1536]{1,0:T(8,128)(2,1)}, bf16[256,1536]{1,0:T(8,128)(2,1)S(1)}, u32[]{:S(2)}, u32[]{:S(2)}) collective-permute-start(bf16[256,1536]{1,0:T(8,128)(2,1)} %get-tuple-element.14), channel_id=1, source_target_pairs={{0,24},{1,25},{2,26},{3,27},{4,28},{5,29},{6,30},{7,31},{8,0},{9,1... | collective-permute-start | bytes 2359304 | tf_op jit(solution)/shard_map/ppermute | solution.py:25
  147.3 17.4 %collective-permute-done.11 = bf16[256,1536]{1,0:T(8,128)(2,1)S(1)} collective-permute-done((bf16[256,1536]{1,0:T(8,128)(2,1)}, bf16[256,1536]{1,0:T(8,128)(2,1)S(1)}, u32[]{:S(2)}, u32[]{:S(2)}) %collective-permute-start.11) | collective-permute-done | bytes 786464 | tf_op jit(solution)/shard_map/ppermute | solution.py:25
  164.7 3.3 %collective-permute-done.12 = bf16[256,1536]{1,0:T(8,128)(2,1)S(1)} collective-permute-done((bf16[256,1536]{1,0:T(8,128)(2,1)}, bf16[256,1536]{1,0:T(8,128)(2,1)S(1)}, u32[]{:S(2)}, u32[]{:S(2)}) %collective-permute-start.12) | collective-permute-done | bytes 786464 | tf_op jit(solution)/shard_map/ppermute | solution.py:25
  169.3 6.9 %all-to-all-start.2 = ((bf16[8,32,1536]{2,1,0:T(8,128)(2,1)}), bf16[8,32,1536]{2,1,0:T(8,128)(2,1)S(1)}, u32[]{:S(2)}, u32[]{:S(2)}) async-start(bf16[8,32,1536]{2,1,0:T(8,128)(2,1)} %bitcast.13), calls=%async_computation.2 | async-start | bytes 1572864 | tf_op jit(solution)/shard_map/all_to_all | solution.py:29
  176.4 21.7 %all-to-all-done.2 = bf16[8,32,1536]{2,1,0:T(8,128)(2,1)S(1)} async-done(((bf16[8,32,1536]{2,1,0:T(8,128)(2,1)}), bf16[8,32,1536]{2,1,0:T(8,128)(2,1)S(1)}, u32[]{:S(2)}, u32[]{:S(2)}) %all-to-all-start.2) | async-done | bytes 786464 | tf_op jit(solution)/shard_map/all_to_all | solution.py:29
  (61 shorter events, 17.1 us)
Async XLA Ops:
  2.0 31.6 %all-to-all-start = ((bf16[8,32,1536]{2,1,0:T(8,128)(2,1)}), bf16[8,32,1536]{2,1,0:T(8,128)(2,1)S(1)}, u32[]{:S(2)}, u32[]{:S(2)}) async-start(bf16[8,32,1536]{2,1,0:T(8,128)(2,1)} %broadcast_in_dim.36), calls=%async_computation | async-start | bytes 1572864 | tf_op jit(solution)/shard_map/all_to_all | solution.py:29
  10.4 6.1 %collective-permute-start.2 = (bf16[32,1536]{1,0:T(8,128)(2,1)S(1)}, bf16[32,1536]{1,0:T(8,128)(2,1)S(1)}, u32[]{:S(2)}, u32[]{:S(2)}) collective-permute-start(bf16[32,1536]{1,0:T(8,128)(2,1)S(1)} %bitcast.50), channel_id=1, source_target_pairs={{0,16},{1,17},{2,18},{3,19},{4,20},{5,21},{6,22},{7,23},{8,24},{9,... | collective-permute-start | bytes 294920 | tf_op jit(solution)/shard_map/ppermute | solution.py:25
  33.5 28.2 %copy-start.2 = (bf16[8,32,1536]{2,1,0:T(8,128)(2,1)}, bf16[8,32,1536]{2,1,0:T(8,128)(2,1)S(1)}, u32[]{:S(2)}) copy-start(bf16[8,32,1536]{2,1,0:T(8,128)(2,1)S(1)} %all-to-all-done) | copy-start | bytes 2359300
  34.6 27.1 %all-to-all-start.1 = ((bf16[8,32,1536]{2,1,0:T(8,128)(2,1)}), bf16[8,32,1536]{2,1,0:T(8,128)(2,1)S(1)}, u32[]{:S(2)}, u32[]{:S(2)}) async-start(bf16[8,32,1536]{2,1,0:T(8,128)(2,1)} %broadcast_in_dim.37), calls=%async_computation.1 | async-start | bytes 1572864 | tf_op jit(solution)/shard_map/all_to_all | solution.py:29
  38.1 23.5 %collective-permute-start = (bf16[256,1536]{1,0:T(8,128)(2,1)S(1)}, bf16[256,1536]{1,0:T(8,128)(2,1)S(1)}, u32[]{:S(2)}, u32[]{:S(2)}) collective-permute-start(bf16[256,1536]{1,0:T(8,128)(2,1)S(1)} %bitcast.44), channel_id=1, source_target_pairs={{0,8},{1,9},{2,10},{3,11},{4,12},{5,13},{6,14},{7,15},{8,16},{9,17... | collective-permute-start | bytes 2359304 | tf_op jit(solution)/shard_map/ppermute | solution.py:25
  39.8 21.9 %collective-permute-start.1 = (bf16[256,1536]{1,0:T(8,128)(2,1)S(1)}, bf16[256,1536]{1,0:T(8,128)(2,1)S(1)}, u32[]{:S(2)}, u32[]{:S(2)}) collective-permute-start(bf16[256,1536]{1,0:T(8,128)(2,1)S(1)} %bitcast.45), channel_id=1, source_target_pairs={{0,24},{1,25},{2,26},{3,27},{4,28},{5,29},{6,30},{7,31},{8,0},{9,1... | collective-permute-start | bytes 2359304 | tf_op jit(solution)/shard_map/ppermute | solution.py:25
  73.1 3.6 %collective-permute-start.3 = (bf16[4,128,1536]{2,1,0:T(8,128)(2,1)}, bf16[4,128,1536]{2,1,0:T(8,128)(2,1)S(1)}, u32[]{:S(2)}, u32[]{:S(2)}) collective-permute-start(bf16[4,128,1536]{2,1,0:T(8,128)(2,1)} %get-tuple-element.12), channel_id=1, source_target_pairs={{0,1},{1,0},{2,3},{3,2},{4,5},{5,4},{6,7},{7,6},{8,9},{9,8},{10,11... | collective-permute-start | bytes 4718600 | tf_op jit(solution)/shard_map/ppermute | solution.py:25
  76.7 6.2 %copy-start.8 = (bf16[1536]{0:T(1024)(128)(2,1)S(1)}, bf16[1536]{0:T(1024)(128)(2,1)}, u32[]{:S(2)}) copy-start(bf16[1536]{0:T(1024)(128)(2,1)} %param.8) | copy-start | bytes 9220
  76.7 6.2 %copy-start.10 = (s32[2,4,12]{2,1,0:T(4,128)S(1)}, s32[2,4,12]{2,1,0:T(4,128)}, u32[]{:S(2)}) copy-start(s32[2,4,12]{2,1,0:T(4,128)} %param.11) | copy-start | bytes 1156
  79.4 12.2 %collective-permute-start.4 = (bf16[128,1536]{1,0:T(8,128)(2,1)}, bf16[128,1536]{1,0:T(8,128)(2,1)S(1)}, u32[]{:S(2)}, u32[]{:S(2)}) collective-permute-start(bf16[128,1536]{1,0:T(8,128)(2,1)} %get-tuple-element.19), channel_id=1, source_target_pairs={{0,2},{1,3},{2,4},{3,5},{4,6},{5,7},{6,0},{7,1},{8,10},{9,11},{10,... | collective-permute-start | bytes 1179656 | tf_op jit(solution)/shard_map/ppermute | solution.py:25
  79.9 20.5 %collective-permute-start.5 = (bf16[128,1536]{1,0:T(8,128)(2,1)S(1)}, bf16[128,1536]{1,0:T(8,128)(2,1)S(1)}, u32[]{:S(2)}, u32[]{:S(2)}) collective-permute-start(bf16[128,1536]{1,0:T(8,128)(2,1)S(1)} %get-tuple-element.21), channel_id=1, source_target_pairs={{0,6},{1,7},{2,0},{3,1},{4,2},{5,3},{6,4},{7,5},{8,14},{9,15},{10,... | collective-permute-start | bytes 1179656 | tf_op jit(solution)/shard_map/ppermute | solution.py:25
  81.5 19.0 %collective-permute-start.6 = (bf16[128,1536]{1,0:T(8,128)(2,1)S(1)}, bf16[128,1536]{1,0:T(8,128)(2,1)S(1)}, u32[]{:S(2)}, u32[]{:S(2)}) collective-permute-start(bf16[128,1536]{1,0:T(8,128)(2,1)S(1)} %get-tuple-element.20), channel_id=1, source_target_pairs={{0,4},{1,5},{2,6},{3,7},{4,0},{5,1},{6,2},{7,3},{8,12},{9,13},{10,... | collective-permute-start | bytes 1179656 | tf_op jit(solution)/shard_map/ppermute | solution.py:25
  104.9 18.0 %collective-permute-start.7 = (bf16[128,1536]{1,0:T(8,128)(2,1)}, bf16[128,1536]{1,0:T(8,128)(2,1)S(1)}, u32[]{:S(2)}, u32[]{:S(2)}) collective-permute-start(bf16[128,1536]{1,0:T(8,128)(2,1)} %get-tuple-element.18), channel_id=1, source_target_pairs={{0,2},{1,3},{2,4},{3,5},{4,6},{5,7},{6,0},{7,1},{8,10},{9,11},{10,... | collective-permute-start | bytes 1179656 | tf_op jit(solution)/shard_map/ppermute | solution.py:25
  106.3 19.9 %collective-permute-start.8 = (bf16[128,1536]{1,0:T(8,128)(2,1)}, bf16[128,1536]{1,0:T(8,128)(2,1)S(1)}, u32[]{:S(2)}, u32[]{:S(2)}) collective-permute-start(bf16[128,1536]{1,0:T(8,128)(2,1)} %get-tuple-element.18), channel_id=1, source_target_pairs={{0,6},{1,7},{2,0},{3,1},{4,2},{5,3},{6,4},{7,5},{8,14},{9,15},{10,... | collective-permute-start | bytes 1179656 | tf_op jit(solution)/shard_map/ppermute | solution.py:25
  106.9 19.3 %collective-permute-start.9 = (bf16[128,1536]{1,0:T(8,128)(2,1)}, bf16[128,1536]{1,0:T(8,128)(2,1)S(1)}, u32[]{:S(2)}, u32[]{:S(2)}) collective-permute-start(bf16[128,1536]{1,0:T(8,128)(2,1)} %get-tuple-element.18), channel_id=1, source_target_pairs={{0,4},{1,5},{2,6},{3,7},{4,0},{5,1},{6,2},{7,3},{8,12},{9,13},{10,... | collective-permute-start | bytes 1179656 | tf_op jit(solution)/shard_map/ppermute | solution.py:25
  126.2 3.5 %copy-start = (bf16[4,128,1536]{2,1,0:T(8,128)(2,1)}, bf16[4,128,1536]{2,1,0:T(8,128)(2,1)S(1)}, u32[]{:S(2)}) copy-start(bf16[4,128,1536]{2,1,0:T(8,128)(2,1)S(1)} %bitcast_dynamic-update-slice_fusion.near) | copy-start | bytes 4718596
  126.2 3.5 %collective-permute-start.10 = (bf16[4,128,1536]{2,1,0:T(8,128)(2,1)S(1)}, bf16[4,128,1536]{2,1,0:T(8,128)(2,1)S(1)}, u32[]{:S(2)}, u32[]{:S(2)}) collective-permute-start(bf16[4,128,1536]{2,1,0:T(8,128)(2,1)S(1)} %bitcast_dynamic-update-slice_fusion.near), channel_id=1, source_target_pairs={{0,1},{1,0},{2,3},{3,2},{4,5},{5,4},{6,7},{7,6},{8,9},{9,8},{10,11... | collective-permute-start | bytes 4718600 | tf_op jit(solution)/shard_map/ppermute | solution.py:25
  140.5 27.5 %copy-start.1 = (f32[256,1536]{1,0:T(8,128)S(1)}, f32[256,1536]{1,0:T(8,128)}, u32[]{:S(2)}) copy-start(f32[256,1536]{1,0:T(8,128)} %get-tuple-element.13) | copy-start | bytes 4718596
  140.5 28.7 %all-to-all-start.3 = ((bf16[8,32,1536]{2,1,0:T(8,128)(2,1)}), bf16[8,32,1536]{2,1,0:T(8,128)(2,1)S(1)}, u32[]{:S(2)}, u32[]{:S(2)}) async-start(bf16[8,32,1536]{2,1,0:T(8,128)(2,1)} %bitcast.47), calls=%async_computation.3 | async-start | bytes 1572864 | tf_op jit(solution)/shard_map/all_to_all | solution.py:29
  144.5 20.3 %collective-permute-start.11 = (bf16[256,1536]{1,0:T(8,128)(2,1)}, bf16[256,1536]{1,0:T(8,128)(2,1)S(1)}, u32[]{:S(2)}, u32[]{:S(2)}) collective-permute-start(bf16[256,1536]{1,0:T(8,128)(2,1)} %get-tuple-element.14), channel_id=1, source_target_pairs={{0,24},{1,25},{2,26},{3,27},{4,28},{5,29},{6,30},{7,31},{8,0},{9,1... | collective-permute-start | bytes 2359304 | tf_op jit(solution)/shard_map/ppermute | solution.py:25
  147.3 20.7 %collective-permute-start.12 = (bf16[256,1536]{1,0:T(8,128)(2,1)}, bf16[256,1536]{1,0:T(8,128)(2,1)S(1)}, u32[]{:S(2)}, u32[]{:S(2)}) collective-permute-start(bf16[256,1536]{1,0:T(8,128)(2,1)} %get-tuple-element.15), channel_id=1, source_target_pairs={{0,8},{1,9},{2,10},{3,11},{4,12},{5,13},{6,14},{7,15},{8,16},{9,17... | collective-permute-start | bytes 2359304 | tf_op jit(solution)/shard_map/ppermute | solution.py:25
  169.3 6.9 %copy-start.9 = (bf16[1536]{0:T(1024)(128)(2,1)S(1)}, bf16[1536]{0:T(1024)(128)(2,1)}, u32[]{:S(2)}) copy-start(bf16[1536]{0:T(1024)(128)(2,1)} %param.10) | copy-start | bytes 9220
  169.3 28.8 %all-to-all-start.2 = ((bf16[8,32,1536]{2,1,0:T(8,128)(2,1)}), bf16[8,32,1536]{2,1,0:T(8,128)(2,1)S(1)}, u32[]{:S(2)}, u32[]{:S(2)}) async-start(bf16[8,32,1536]{2,1,0:T(8,128)(2,1)} %bitcast.13), calls=%async_computation.2 | async-start | bytes 1572864 | tf_op jit(solution)/shard_map/all_to_all | solution.py:29
  176.3 21.9 %collective-permute-start.13 = (bf16[32,1536]{1,0:T(8,128)(2,1)S(1)}, bf16[32,1536]{1,0:T(8,128)(2,1)S(1)}, u32[]{:S(2)}, u32[]{:S(2)}) collective-permute-start(bf16[32,1536]{1,0:T(8,128)(2,1)S(1)} %reduce_sum.22), channel_id=1, source_target_pairs={{0,16},{1,17},{2,18},{3,19},{4,20},{5,21},{6,22},{7,23},{8,24},{9,... | collective-permute-start | bytes 294920 | tf_op jit(solution)/shard_map/ppermute | solution.py:25
  (8 other events, 8.4 us)
